TPU v7x, 256 devices: a whole 4x4x8 slice. The times are simulated.
256 devices in a mesh: band: 64 (over x, y_hi, z), chan: 4 (over y_lo, core).
Axes of the slice: x: 4, y: 4 (y_hi: 2, y_lo: 2; y = y_hi * 2 + y_lo), z: 8, core: 2. Of those that a mesh axis runs over, the one named last changes fastest.
Arguments:
- atmos: bfloat16 [256, 368640], P('chan', 'band'), may hold values from -6 to 6
- kernels: float32 [1, 3, 256], P(None, None, 'chan'), may hold values from -3 to 3
- w_one: bfloat16 [1, 256, 1024], P(None, None, 'chan'), may hold values from -0.375 to 0.375
- w_two: bfloat16 [1, 1024, 256], P(None, 'chan'), may hold values from -0.1875 to 0.1875
- w_flux: bfloat16 [256, 128], P('chan'), may hold values from -0.375 to 0.375
- sea_mask: int32 [368640], P('band'), may hold values 0 or 1
- route: int32 [2880, 1], P('band'), may hold values from 0 to 63; in each aligned block of 45 rows (0 to 44, 45 to 89, ...) at most 2 rows name the same one
- ocean_state: bfloat16 [128, 64, 128, 128], P(None, 'band'), may hold values from -6 to 6
- ct_atmos: bfloat16 [256, 368640], P('chan', 'band'), may hold values from -6 to 6
- ct_ocean: bfloat16 [128, 64, 128, 128], P(None, 'band'), may hold values from -6 to 6
- wo_one: bfloat16 [256, 512], P(None, 'chan'), may hold values from -0.375 to 0.375
- wo_two: bfloat16 [512, 128], P('chan'), may hold values from -0.25 to 0.25
Outputs:
- d_atmos: bfloat16 [256, 368640], P('chan', 'band')
- d_kernels: float32 [1, 3, 256], P(None, None, 'chan')
- d_w_one: float32 [1, 256, 1024], P(None, None, 'chan')
- d_w_two: float32 [1, 1024, 256], P(None, 'chan')
- d_w_flux: float32 [256, 128], P('chan')
- d_ocean_state: bfloat16 [128, 64, 128, 128], P('chan', 'band')
- d_wo_one: float32 [256, 512], P(None, 'chan')
- d_wo_two: float32 [512, 128], P('chan')
Inputs may be any that keep to these rules, and one draw needn't show every extreme that they name: route[k, 0] is the ocean tile that takes block k; among the 45 blocks of one row group no tile is named more than 2 times, a bound that some block reaches.
All inputs are finite; a program needn't handle non-finite values. No bound on the sum of `sea_mask` on one device may be relied on, other than what follows from the above.
Results may differ from a plain program's by a relative error of at most 0.028.
Values may be sent and summed in bfloat16 or wider, within the bound.
A program may use at most 128 MiB of HBM per device.

v0:
```python
import jax
import jax.numpy as jnp
from jax import lax
from jax.sharding import PartitionSpec as P

PTS = 128
LON = 1440
LAYERS = 1


def extended(cells, sides, width):
    for axis, dim in sides:
        count = lax.axis_size(axis)
        ends = count - 1
        head = lax.slice_in_dim(cells, 0, width, axis=dim)
        tail = lax.slice_in_dim(cells, cells.shape[dim] - width, cells.shape[dim], axis=dim)
        cells = jnp.concatenate(
            [
                lax.ppermute(tail, axis, [(i, (i + 1) % count) for i in range(ends)]),
                cells,
                lax.ppermute(head, axis, [((i + 1) % count, i) for i in range(ends)]),
            ],
            axis=dim,
        )
    return cells


def for_sending(x):
    return jax.tree.map(lambda a: a.astype(jnp.bfloat16) if a.dtype == jnp.float32 else a, x)


def silu_grad(values):
    sigma = jax.nn.sigmoid(values)
    return sigma * (1.0 + values * (1.0 - sigma))


def contract(left, right, left_dim, right_dim):
    return lax.dot_general(
        left, right, (((left_dim,), (right_dim,)), ((), ())), preferred_element_type=jnp.float32
    )


def convolve(padded, kernel_taps):
    return (
        kernel_taps[0][:, None] * padded[:, : -2 * LON]
        + kernel_taps[1][:, None] * padded[:, LON:-LON]
        + kernel_taps[2][:, None] * padded[:, 2 * LON :]
    )


def row_halo(field):
    return extended(field, (("band", 1),), LON)


def whole_chan(field):
    return lax.all_gather(field, "chan", axis=0, tiled=True)


def chan_share(terms):
    return jax.tree.map(
        lambda part: part.astype(jnp.float32),
        lax.psum_scatter(for_sending(terms), "chan", scatter_dimension=0, tiled=True),
    )


def couple(blocks):
    return lax.all_to_all(blocks, "band", split_axis=1, concat_axis=1, tiled=True)


def pack_blocks(forcing, select):
    return jnp.einsum("pbo,bs->pso", forcing, select, preferred_element_type=jnp.float32).astype(
        jnp.bfloat16
    )


def local(
    atmos,
    kernels,
    w_one,
    w_two,
    w_flux,
    sea_mask,
    route,
    ocean_state,
    ct_atmos,
    ct_ocean,
    wo_one,
    wo_two,
):
    chan_count = lax.axis_size("chan")
    chan_index = lax.axis_index("chan")
    band_count = lax.axis_size("band")
    chan_width, grid_points = atmos.shape
    blocks = grid_points // PTS
    slot_total = ocean_state.shape[2]
    capacity = slot_total // band_count
    ocean_width = ocean_state.shape[3]
    quarter = PTS // chan_count
    state = atmos
    layer_idx = 0
    padded = row_halo(state)
    mixed_in = convolve(padded, kernels[layer_idx]).astype(jnp.bfloat16)
    full_in = whole_chan(mixed_in)
    pre_act = contract(w_one[layer_idx], full_in, 0, 0)
    hidden_layer = jax.nn.silu(pre_act).astype(jnp.bfloat16)
    update = chan_share(contract(w_two[layer_idx], hidden_layer, 0, 0))
    saved = [(padded, full_in, pre_act, hidden_layer)]
    state = (state.astype(jnp.float32) + update).astype(jnp.bfloat16)
    final_blocks = state.reshape(chan_width, blocks, PTS)
    flux_terms = jnp.einsum("cbp,co->pbo", final_blocks, w_flux, preferred_element_type=jnp.float32)
    mask_blocks = sea_mask.reshape(blocks, PTS).T.astype(jnp.float32)
    mask_share = lax.dynamic_slice_in_dim(mask_blocks, chan_index * quarter, quarter, 0)
    target = route[:, 0]
    order = jnp.arange(blocks, dtype=jnp.int32)
    earlier = (target[None, :] == target[:, None]) & (order[None, :] < order[:, None])
    rank = jnp.sum(earlier.astype(jnp.int32), axis=1)
    slot_of = target * capacity + rank
    select = (slot_of[:, None] == jnp.arange(slot_total, dtype=jnp.int32)[None, :]).astype(
        jnp.bfloat16
    )
    total_flux = lax.psum(flux_terms.astype(jnp.bfloat16), "chan").astype(jnp.float32)
    forcing = (total_flux * mask_blocks[:, :, None]).astype(jnp.bfloat16)
    arrived = couple(pack_blocks(forcing, select).reshape(PTS, band_count, capacity, ocean_width))
    full_forcing = arrived.reshape(PTS, slot_total, ocean_width)
    cotan_share = lax.dynamic_slice_in_dim(ct_ocean[:, 0], chan_index * quarter, quarter, 0)
    total_rows = PTS * slot_total
    own_state = ocean_state[:, 0].reshape(total_rows, ocean_width)
    own_forcing = full_forcing.reshape(total_rows, ocean_width)
    own_cotan = ct_ocean[:, 0].reshape(total_rows, ocean_width)
    upper = wo_one[:ocean_width]
    lower = wo_one[ocean_width:]
    ocean_pre = contract(own_state, upper, 1, 0) + contract(own_forcing, lower, 1, 0)
    ocean_act = jax.nn.silu(ocean_pre).astype(jnp.bfloat16)
    ocean_grad = (contract(own_cotan, wo_two, 1, 1) * silu_grad(ocean_pre)).astype(jnp.bfloat16)
    grad_wo_two = contract(ocean_act, own_cotan, 0, 0)
    grad_wo_one = jnp.concatenate(
        [contract(own_state, ocean_grad, 0, 0), contract(own_forcing, ocean_grad, 0, 0)], axis=0
    )
    state_terms = contract(ocean_grad, upper, 1, 1).reshape(PTS, slot_total, ocean_width)
    forcing_terms = contract(ocean_grad, lower, 1, 1).reshape(PTS, slot_total, ocean_width)
    state_sum, forcing_sum = chan_share((state_terms, forcing_terms))
    d_ocean_state = (state_sum + cotan_share.astype(jnp.float32)).astype(jnp.bfloat16)[:, None]
    returned = couple(
        forcing_sum.astype(jnp.bfloat16).reshape(quarter, band_count, capacity, ocean_width)
    )
    back_blocks = jnp.einsum(
        "pso,bs->pbo",
        returned.reshape(quarter, slot_total, ocean_width),
        select,
        preferred_element_type=jnp.float32,
    )
    d_flux_share = (back_blocks * mask_share[:, :, None]).astype(jnp.bfloat16)
    d_flux = whole_chan(d_flux_share)
    grad_flux = jnp.einsum("cbp,pbo->co", final_blocks, d_flux, preferred_element_type=jnp.float32)
    back_state = jnp.einsum(
        "pbo,co->cbp", d_flux, w_flux, preferred_element_type=jnp.float32
    ).reshape(atmos.shape)
    cotan = (ct_atmos.astype(jnp.float32) + back_state).astype(jnp.bfloat16)
    tap_grads = [None] * LAYERS
    one_grads = [None] * LAYERS
    two_grads = [None] * LAYERS
    for layer_idx in reversed(range(LAYERS)):
        padded, full_in, pre_act, hidden_layer = saved[layer_idx]
        full_cotan = whole_chan(cotan)
        hidden_layer_gradient = (
            contract(w_two[layer_idx], full_cotan, 1, 0) * silu_grad(pre_act)
        ).astype(jnp.bfloat16)
        two_grads[layer_idx] = contract(hidden_layer, full_cotan, 1, 1)
        one_grads[layer_idx] = contract(full_in, hidden_layer_gradient, 1, 1)
        conv_grad = chan_share(contract(w_one[layer_idx], hidden_layer_gradient, 1, 0)).astype(
            jnp.bfloat16
        )
        conv_pad = row_halo(conv_grad)
        conv_float = conv_grad.astype(jnp.float32)
        tap_grads[layer_idx] = jnp.stack(
            [
                jnp.sum(
                    padded[:, offset * LON : offset * LON + grid_points].astype(jnp.float32)
                    * conv_float,
                    axis=1,
                )
                for offset in range(3)
            ]
        )
        kernel_taps = kernels[layer_idx]
        spread = (
            kernel_taps[0][:, None] * conv_pad[:, 2 * LON :]
            + kernel_taps[1][:, None] * conv_pad[:, LON:-LON]
            + kernel_taps[2][:, None] * conv_pad[:, : -2 * LON]
        )
        cotan = (cotan.astype(jnp.float32) + spread).astype(jnp.bfloat16)
    summed = lax.psum(
        (
            jnp.stack(tap_grads),
            jnp.stack(one_grads),
            jnp.stack(two_grads),
            grad_flux,
            grad_wo_one,
            grad_wo_two,
        ),
        "band",
    )
    return (cotan, summed[0], summed[1], summed[2], summed[3], d_ocean_state, summed[4], summed[5])


def solution(mesh):
    in_specs = (
        P("chan", "band"),
        P(None, None, "chan"),
        P(None, None, "chan"),
        P(None, "chan", None),
        P("chan", None),
        P("band"),
        P("band", None),
        P(None, "band", None, None),
        P("chan", "band"),
        P(None, "band", None, None),
        P(None, "chan"),
        P("chan", None),
    )
    out_specs = (
        P("chan", "band"),
        P(None, None, "chan"),
        P(None, None, "chan"),
        P(None, "chan", None),
        P("chan", None),
        P("chan", "band", None, None),
        P(None, "chan"),
        P("chan", None),
    )
    return jax.shard_map(local, mesh=mesh, in_specs=in_specs, out_specs=out_specs, check_vma=False)
```

profile of v0, /device:TPU:8, one launch (start us, length us, event | category | flops | bytes accessed | tf_op | source)
XLA Modules:
  0.0 1253.6 jit_solution(2394136820084701214)
XLA Ops:
  7.2 1.2 fusion.49
  8.4 3.8 collective-permute-start
  12.2 1.3 collective-permute-start.1
  14.2 2.1 collective-permute-done
  16.4 4.3 collective-permute-done.1
  20.7 3.4 fusion.10
  24.2 41.4 %all-gather.4.cloned.1.call-done = bf16[256,5760]{1,0:T(8,128)(2,1)} async-done(((bf16[64,5760]{1,0:T(8,128)(2,1)}), bf16[256,5760]{1,0:T(8,128)(2,1)}) %all-gather.4.cloned.1.call-update) | async-done | bytes 2949136 | tf_op jit(solution)/shard_map/all_gather | solution.py:56
  65.5 6.1 multiply_convert_fusion.1
  71.6 1.6 copy-done.8
  73.2 1.8 fusion.3
  75.0 3.8 copy.101
  78.9 38.7 %reduce-scatter.13.cloned.1.call-done = bf16[64,5760]{1,0:T(8,128)(2,1)} async-done(((bf16[256,5760]{1,0:T(8,128)(2,1)}), bf16[64,5760]{1,0:T(8,128)(2,1)}) %reduce-scatter.13.cloned.1.call-update) | async-done | bytes 737296 | tf_op jit(solution)/shard_map/reduce_scatter | solution.py:62
  117.6 2.9 fusion.20
  120.7 54.0 %all-reduce.5.cloned.1.call-done = bf16[128,45,128]{2,0,1:T(8,128)(2,1)} async-done(((bf16[128,45,128]{2,0,1:T(8,128)(2,1)}), bf16[128,45,128]{2,0,1:T(8,128)(2,1)}) %all-reduce.5.cloned.1.call-update) | async-done | bytes 1474576 | tf_op jit(solution)/shard_map/psum | solution.py:121
  174.7 2.1 multiply_convert_fusion.3
  176.8 1.5 convolution_convert_fusion.4
  178.3 6.7 copy.85
  185.0 12.9 %all-to-all-start = ((bf16[128,64,2,128]{3,2,0,1:T(2,128)(2,1)}), bf16[128,64,2,128]{3,2,0,1:T(2,128)(2,1)}, u32[]{:S(2)}, u32[]{:S(2)}) async-start(bf16[128,64,2,128]{3,2,0,1:T(2,128)(2,1)} %copy.85), calls=%async_computation | async-start | bytes 8388608 | tf_op jit(solution)/shard_map/all_to_all | solution.py:67
  198.1 6.7 fusion.36
  204.8 91.5 %all-to-all-done = bf16[128,64,2,128]{3,2,0,1:T(2,128)(2,1)} async-done(((bf16[128,64,2,128]{3,2,0,1:T(2,128)(2,1)}), bf16[128,64,2,128]{3,2,0,1:T(2,128)(2,1)}, u32[]{:S(2)}, u32[]{:S(2)}) %all-to-all-start) | async-done | bytes 4194336 | tf_op jit(solution)/shard_map/all_to_all | solution.py:67
  296.3 6.9 copy.86
  303.3 6.2 convolution_add_fusion
  309.5 3.3 copy-done.5
  312.8 3.8 fusion
  316.6 1.2 convolution_convert_fusion.1
  317.8 0.8 copy-done.1
  318.6 4.7 copy.87
  323.3 42.0 %reduce-scatter.9.cloned.1.call-done = bf16[32,128,128]{2,0,1:T(8,128)(2,1)} async-done(((bf16[128,128,128]{2,0,1:T(8,128)(2,1)}), bf16[32,128,128]{2,0,1:T(8,128)(2,1)}) %reduce-scatter.9.cloned.1.call-update) | async-done | bytes 1048592 | tf_op jit(solution)/shard_map/reduce_scatter | solution.py:62
  365.3 3.3 copy.88
  368.6 13.2 %all-to-all-start.1 = ((bf16[32,64,2,128]{3,2,0,1:T(2,128)(2,1)}), bf16[32,64,2,128]{3,2,0,1:T(2,128)(2,1)S(1)}, u32[]{:S(2)}, u32[]{:S(2)}) async-start(bf16[32,64,2,128]{3,2,0,1:T(2,128)(2,1)} %copy.88), calls=%async_computation.2 | async-start | bytes 2097152 | tf_op jit(solution)/shard_map/all_to_all | solution.py:67
  382.0 30.6 %all-to-all-done.1 = bf16[32,64,2,128]{3,2,0,1:T(2,128)(2,1)S(1)} async-done(((bf16[32,64,2,128]{3,2,0,1:T(2,128)(2,1)}), bf16[32,64,2,128]{3,2,0,1:T(2,128)(2,1)S(1)}, u32[]{:S(2)}, u32[]{:S(2)}) %all-to-all-start.1) | async-done | bytes 1048608 | tf_op jit(solution)/shard_map/all_to_all | solution.py:67
  412.6 1.1 copy.89
  414.0 0.8 copy.91
  414.9 21.0 %all-gather.6.cloned.1.call-done = bf16[128,45,128]{2,0,1:T(8,128)(2,1)} async-done(((bf16[32,45,128]{2,0,1:T(8,128)(2,1)}), bf16[128,45,128]{2,0,1:T(8,128)(2,1)}) %all-gather.6.cloned.1.call-update) | async-done | bytes 1474576 | tf_op jit(solution)/shard_map/all_gather | solution.py:56
  436.0 2.0 convolution_bitcast_fusion.2
  438.0 1.0 fusion.19
  439.1 5.5 convolution_convert_fusion
  444.6 33.8 %all-gather.8.cloned.1.call-done = bf16[256,5760]{1,0:T(8,128)(2,1)} async-done(((bf16[64,5760]{1,0:T(8,128)(2,1)}), bf16[256,5760]{1,0:T(8,128)(2,1)}) %all-gather.8.cloned.1.call-update) | async-done | bytes 2949136 | tf_op jit(solution)/shard_map/all_gather | solution.py:56
  478.4 5.3 fusion.2
  483.8 1.6 copy-done.10
  485.4 1.0 fusion.4
  486.4 3.8 copy.103
  490.3 4.9 fusion.50
  495.2 1.7 copy-done.4
  496.9 1.3 convolution_bitcast_fusion.6
  499.1 6.5 fusion.5
  505.6 24.4 %reduce-scatter.11.cloned.1.call-done = bf16[32,128,128]{2,1,0:T(8,128)(2,1)} async-done(((bf16[128,128,128]{2,1,0:T(8,128)(2,1)}), bf16[32,128,128]{2,1,0:T(8,128)(2,1)}) %reduce-scatter.11.cloned.1.call-update) | async-done | bytes 1048592 | tf_op jit(solution)/shard_map/reduce_scatter | solution.py:62
  530.0 3.0 fusion.23
  533.0 3.7 convolution_bitcast_fusion.4
  536.7 1.7 convolution_bitcast_fusion.5
  538.4 33.0 %reduce-scatter.15.cloned.1.call-done = bf16[64,5760]{1,0:T(8,128)(2,1)} async-done(((bf16[256,5760]{1,0:T(8,128)(2,1)}), bf16[64,5760]{1,0:T(8,128)(2,1)}) %reduce-scatter.15.cloned.1.call-update) | async-done | bytes 737296 | tf_op jit(solution)/shard_map/reduce_scatter | solution.py:62
  571.3 1.2 fusion.48
  572.5 1.3 collective-permute-start.2
  573.8 4.8 collective-permute-start.3
  578.7 1.5 convolution_bitcast_fusion.7
  580.2 1.7 collective-permute-done.2
  581.9 1.2 collective-permute-done.3
  583.1 3.1 fusion.16
  586.2 360.3 %all-reduce = (f32[1,3,64]{2,1,0:T(4,128)S(1)}, f32[64,128]{1,0:T(8,128)}) all-reduce(f32[1,3,64]{2,1,0:T(4,128)S(1)} %maximum_bitcast_fusion, f32[64,128]{1,0:T(8,128)S(1)} %convolution_bitcast_fusion.7), channel_id=1, replica_groups=mesh['band'=64,'chan'=4] {'band'}, use_global_device_ids=true, to_apply=%region_8.9 | all-reduce | flops 8384 | bytes 67072 | tf_op jit(solution)/shard_map/psum | solution.py:192
  947.0 293.2 %all-reduce.7.cloned.1.call-done = (f32[1,256,256]{2,1,0:T(8,128)}, f32[1,256,256]{2,1,0:T(8,128)}, f32[256,128]{1,0:T(8,128)}, f32[128,128]{1,0:T(8,128)}) async-done(((f32[1,256,256]{2,1,0:T(8,128)}, f32[1,256,256]{2,1,0:T(8,128)}, f32[256,128]{1,0:T(8,128)}, f32[128,128]{1,0:T(8,128)}), (f32[1,256,256]{2,1,0:T(8,128)}, f32[1,256,256]{2,1,0:T(8,128)}, f32[256,128]{1,0:T(8,128)}, ...) | async-done | bytes 720912 | tf_op jit(solution)/shard_map/psum | solution.py:192
  1240.3 1.7 copy.123
  1241.9 1.7 copy.124
  1243.6 1.6 copy.125
  1245.2 1.5 copy.126
  (73 shorter events, 3.6 us)
Async XLA Ops:
  7.2 58.4 %copy-start = (bf16[1,256,256]{2,1,0:T(8,128)(2,1)S(1)}, bf16[1,256,256]{2,1,0:T(8,128)(2,1)}, u32[]{:S(2)}) copy-start(bf16[1,256,256]{2,1,0:T(8,128)(2,1)} %param.14) | copy-start | bytes 393220
  7.2 58.4 %all-gather.4.cloned.1.call-start = ((), (), s32[]{:S(2)}) async-start(), calls=%async_computation.6 | async-start | bytes 3686400 | tf_op jit(solution)/shard_map/all_gather | solution.py:56
  8.4 8.0 collective-permute-start
  12.2 8.4 collective-permute-start.1
  24.1 93.5 %reduce-scatter.13.cloned.1.call-start = ((), (), s32[]{:S(2)}) async-start(), calls=%async_computation.12 | async-start | bytes 3686400 | tf_op jit(solution)/shard_map/reduce_scatter | solution.py:62
  71.6 1.6 copy-start.8
  78.8 38.8 %copy-start.6 = (bf16[64,5760]{1,0:T(8,128)(2,1)S(1)}, bf16[64,5760]{1,0:T(8,128)(2,1)}, u32[]{:S(2)}) copy-start(bf16[64,5760]{1,0:T(8,128)(2,1)} %param.12) | copy-start | bytes 2211844
  78.8 38.8 %copy-start.20 = (bf16[64,128]{1,0:T(8,128)(2,1)S(1)}, bf16[64,128]{1,0:T(8,128)(2,1)}, u32[]{:S(2)}) copy-start(bf16[64,128]{1,0:T(8,128)(2,1)} %param.16) | copy-start | bytes 49156
  78.8 41.7 %copy-start.24 = (s32[45,1]{0,1:T(1,128)S(1)}, s32[45,1]{0,1:T(1,128)}, u32[]{:S(2)}) copy-start(s32[45,1]{0,1:T(1,128)} %param.18) | copy-start | bytes 544
  78.8 41.9 %copy-start.21 = (s32[5760]{0:T(1024)S(1)}, s32[5760]{0:T(1024)}, u32[]{:S(2)}) copy-start(s32[5760]{0:T(1024)} %param.17) | copy-start | bytes 69124
  78.8 95.9 %all-reduce.5.cloned.1.call-start = ((), (), s32[]{:S(2)}) async-start(), calls=%async_computation.7 | async-start | bytes 2949120 | tf_op jit(solution)/shard_map/psum | solution.py:121
  185.0 13.1 %copy-start.16 = (bf16[256,128]{1,0:T(8,128)(2,1)S(1)}, bf16[256,128]{1,0:T(8,128)(2,1)}, u32[]{:S(2)}) copy-start(bf16[256,128]{1,0:T(8,128)(2,1)} %param.22) | copy-start | bytes 196612
  185.0 111.3 %all-to-all-start = ((bf16[128,64,2,128]{3,2,0,1:T(2,128)(2,1)}), bf16[128,64,2,128]{3,2,0,1:T(2,128)(2,1)}, u32[]{:S(2)}, u32[]{:S(2)}) async-start(bf16[128,64,2,128]{3,2,0,1:T(2,128)(2,1)} %copy.85), calls=%async_computation | async-start | bytes 8388608 | tf_op jit(solution)/shard_map/all_to_all | solution.py:67
  197.9 167.4 %reduce-scatter.9.cloned.1.call-start = ((), (), s32[]{:S(2)}) async-start(), calls=%async_computation.8 | async-start | bytes 5242880 | tf_op jit(solution)/shard_map/reduce_scatter | solution.py:62
  303.2 6.3 copy-start.3
  303.2 9.5 copy-start.17
  303.3 9.5 copy-start.23
  309.5 3.3 copy-start.5
  316.6 2.0 copy-start.1
  368.6 44.0 %all-to-all-start.1 = ((bf16[32,64,2,128]{3,2,0,1:T(2,128)(2,1)}), bf16[32,64,2,128]{3,2,0,1:T(2,128)(2,1)S(1)}, u32[]{:S(2)}, u32[]{:S(2)}) async-start(bf16[32,64,2,128]{3,2,0,1:T(2,128)(2,1)} %copy.88), calls=%async_computation.2 | async-start | bytes 2097152 | tf_op jit(solution)/shard_map/all_to_all | solution.py:67
  381.8 54.2 %all-gather.6.cloned.1.call-start = ((), (), s32[]{:S(2)}) async-start(), calls=%async_computation.9 | async-start | bytes 1843200 | tf_op jit(solution)/shard_map/all_gather | solution.py:56
  413.7 24.3 %copy-start.15 = (bf16[64,5760]{1,0:T(8,128)(2,1)S(1)}, bf16[64,5760]{1,0:T(8,128)(2,1)}, u32[]{:S(2)}) copy-start(bf16[64,5760]{1,0:T(8,128)(2,1)} %param.20) | copy-start | bytes 2211844
  414.9 63.5 %all-gather.8.cloned.1.call-start = ((), (), s32[]{:S(2)}) async-start(), calls=%async_computation.10 | async-start | bytes 3686400 | tf_op jit(solution)/shard_map/all_gather | solution.py:56
  439.0 91.0 %reduce-scatter.11.cloned.1.call-start = ((), (), s32[]{:S(2)}) async-start(), calls=%async_computation.11 | async-start | bytes 5242880 | tf_op jit(solution)/shard_map/reduce_scatter | solution.py:62
  444.5 33.9 %copy-start.19 = (bf16[1,256,256]{2,1,0:T(8,128)(2,1)S(1)}, bf16[1,256,256]{2,1,0:T(8,128)(2,1)}, u32[]{:S(2)}) copy-start(bf16[1,256,256]{2,1,0:T(8,128)(2,1)} %param.15) | copy-start | bytes 393220
  444.6 126.8 %reduce-scatter.15.cloned.1.call-start = ((), (), s32[]{:S(2)}) async-start(), calls=%async_computation.13 | async-start | bytes 3686400 | tf_op jit(solution)/shard_map/reduce_scatter | solution.py:62
  483.8 1.6 copy-start.10
  490.2 750.1 %all-reduce.7.cloned.1.call-start = ((), (), s32[]{:S(2)}) async-start(), calls=%async_computation.14 | async-start | bytes 1441792 | tf_op jit(solution)/shard_map/psum | solution.py:192
  490.2 4.9 copy-start.2
  490.2 6.7 copy-start.4
  496.9 2.2 copy-start.18
  505.6 27.4 %copy-start.9 = (bf16[256,5760]{0,1:T(8,128)(2,1)S(1)}, bf16[256,5760]{0,1:T(8,128)(2,1)}, u32[]{:S(2)}) copy-start(bf16[256,5760]{0,1:T(8,128)(2,1)} %copy-done.8) | copy-start | bytes 8847364
  533.0 3.7 copy-start.11
  533.0 3.7 copy-start.22
  536.7 42.0 %copy-start.7 = (bf16[64,5760]{1,0:T(8,128)(2,1)S(1)}, bf16[64,5760]{1,0:T(8,128)(2,1)}, u32[]{:S(2)}) copy-start(bf16[64,5760]{1,0:T(8,128)(2,1)} %param.12) | copy-start | bytes 2211844
  536.7 42.0 %copy-start.13 = (bf16[128,45,128]{2,0,1:T(8,128)(2,1)S(1)}, bf16[128,45,128]{2,0,1:T(8,128)(2,1)}, u32[]{:S(2)}) copy-start(bf16[128,45,128]{2,0,1:T(8,128)(2,1)} %all-gather.6.cloned.1.call-done) | copy-start | bytes 4423684
  538.3 44.7 %copy-start.12 = (bf16[64,5760]{1,0:T(8,128)(2,1)S(1)}, bf16[64,5760]{1,0:T(8,128)(2,1)}, u32[]{:S(2)}) copy-start(bf16[64,5760]{1,0:T(8,128)(2,1)} %fusion.19) | copy-start | bytes 2211844
  571.3 11.8 copy-start.14
  572.5 9.4 collective-permute-start.2
  573.8 9.2 collective-permute-start.3
Sparse Core Ops, SparseCore 0:
  24.2 41.2 all-gather.3
  78.9 38.6 reduce-scatter.12
  120.6 54.0 all-reduce.4
  323.4 41.7 reduce-scatter.8
  415.0 20.9 all-gather.5
  439.1 39.2 all-gather.7
  481.1 48.8 reduce-scatter.10
  532.6 38.7 reduce-scatter.14
  575.0 665.1 all-reduce.6
where the time goes:
time: 1260 us; the launch traced here: 1250 us
  waiting for transfers between devices  713 us (57%)
  blocking collectives  360 us (29%)
  matrix products  63.9 us (5%)
  local copies, waits for them, and re-layouts  50.4 us (4%)
  starting transfers between devices  37.9 us (3%)
  between operations  14.6 us (1%)
  other arithmetic  13.4 us (1%)
    psum x1, blocking collectives, local(): lax.psum((jnp.stack(tap_grads), jnp.stack(one_grads), jnp.stack(two_grads...  360 us
    psum x1, waiting for transfers between devices, local(): lax.psum((jnp.stack(tap_grads), jnp.stack(one_grads), jnp.stack(two_grads...  293 us
    reduce_scatter x4, waiting for transfers between devices, chan_share(): lax.psum_scatter(for_sending(terms), 'chan', scatter_dimension=0, tiled=T...  138 us
    all_to_all x2, waiting for transfers between devices, couple(): lax.all_to_all(blocks, 'band', split_axis=1, concat_axis=1, tiled=True)  122 us
    all_gather x3, waiting for transfers between devices, whole_chan(): return lax.all_gather(field, 'chan', axis=0, tiled=True)  96.2 us
    dot_general x14, matrix products, contract(): lax.dot_general(left, right, (((left_dim,), (right_dim,)), ((), ())), pre...  55.7 us
    psum x1, waiting for transfers between devices, local(): lax.psum(flux_terms.astype(jnp.bfloat16), 'chan').astype(jnp.float32)  54 us
    all_to_all x2, starting transfers between devices, couple(): lax.all_to_all(blocks, 'band', split_axis=1, concat_axis=1, tiled=True)  26.1 us
  transfers between devices with their start and end apart: 15, of which 15 were waited for; matrix products, arithmetic and copies ran while one was open for 4% of the time, Pallas kernels for 0%

commit v1 on v0

v1 whole, which is shorter than its diff:
```python
import functools

import jax
import jax.numpy as jnp
from jax import lax
from jax.experimental import pallas as pl
from jax.experimental.pallas import tpu as pltpu
from jax.sharding import PartitionSpec as P

PTS = 128
LON = 1440
MESH = pl.DeviceIdType.MESH
F32 = jnp.float32
BF16 = jnp.bfloat16
VMEM = pltpu.VMEM
DMA = pltpu.SemaphoreType.DMA
ZLEN = 8
LIMIT = 56 * 1024 * 1024


def nn(a, b):
    return lax.dot_general(a, b, (((1,), (0,)), ((), ())), preferred_element_type=F32)


def tn(a, b):
    return lax.dot_general(a, b, (((0,), (0,)), ((), ())), preferred_element_type=F32)


def nt(a, b):
    return lax.dot_general(a, b, (((1,), (1,)), ((), ())), preferred_element_type=F32)


def sigmoid(v):
    return 0.5 * jnp.tanh(0.5 * v) + 0.5


def place():
    b, c = lax.axis_index("band"), lax.axis_index("chan")
    mate = (c // 2) * 2 + (1 - c % 2)
    return b, c, mate, (c + 2) % 4, (mate + 2) % 4


def send(src, dst, ssem, rsem, b, c):
    copy = pltpu.make_async_remote_copy(
        src_ref=src,
        dst_ref=dst,
        send_sem=ssem,
        recv_sem=rsem,
        device_id=(b, c),
        device_id_type=MESH,
    )
    copy.start()
    return copy


def drain(ref, sem):
    pltpu.make_async_copy(ref, ref, sem).wait()


def signal(b, c):
    pl.semaphore_signal(
        pltpu.get_barrier_semaphore(), inc=1, device_id=(b, c), device_id_type=MESH
    )


def shifted(ref, start, extra, width):
    wide = ref[:, start : start + width + 128].astype(F32)
    return pltpu.roll(wide, width + 128 - extra, axis=1)[:, :width]


def forward_kernel(
    atmos, taps, w_one, w_two, w_flux,
    ext, zb, al, w1, w2, wf, fp,
    zc, ab, fx,
    hs, hr, ws, wr, zs, zr, as_, ar, fs, fr,
):
    b, c, mate, across, diag = place()
    bands = lax.axis_size("band")
    up, down = (b + bands - 1) % bands, (b + 1) % bands
    rows, points = atmos.shape
    share = zb.shape[1]
    quarter = fp.shape[1]
    signal(up, c)
    signal(down, c)
    for d in (1, 2, 3):
        signal(b, (c + d) % 4)
    pl.semaphore_wait(pltpu.get_barrier_semaphore(), 5)

    halo = [
        send(atmos.at[:, points - share :], ext.at[:, :share], hs.at[0], hr.at[0], down, c),
        send(atmos.at[:, :share], ext.at[:, share + points :], hs.at[1], hr.at[1], up, c),
    ]
    mine = pl.ds(pl.multiple_of(c * rows, rows), rows)
    theirs = pl.ds(pl.multiple_of(across * rows, rows), rows)
    sources = (w_one, w_two, w_flux)
    slots = (w1.at[c], w2.at[c], wf.at[mine, :])
    far = (w1.at[across], w2.at[across], wf.at[theirs, :])
    first, second = [], []
    for i in range(3):
        second.append(send(sources[i], slots[i], ws.at[1, i], wr.at[1, i], b, across))
        first.append(send(sources[i], slots[i], ws.at[0, i], wr.at[0, i], b, mate))
    w1[c] = w_one[...]
    w2[c] = w_two[...]
    wf[mine, :] = w_flux[...]
    ext[:, share : share + points] = atmos[...]
    zc[:, points:] = jnp.zeros((rows, zc.shape[1] - points), BF16)
    for copy in halo:
        copy.wait()

    @pl.when(b == 0)
    def _():
        ext[:, :share] = jnp.zeros((rows, share), BF16)

    @pl.when(b == bands - 1)
    def _():
        ext[:, share + points :] = jnp.zeros((rows, share), BF16)

    t0, t1, t2 = taps[:, 0:1], taps[:, 1:2], taps[:, 2:3]
    width = 384
    low = share - LON
    high = share + LON
    for at in range(0, points, width):
        zc[:, at : at + width] = (
            t0 * shifted(ext, at + low // 128 * 128, low % 128, width)
            + t1 * ext[:, at + share : at + share + width].astype(F32)
            + t2 * shifted(ext, at + high // 128 * 128, high % 128, width)
        ).astype(BF16)
    zcopies, acopies = [], []
    for d in (2, 1, 3):
        to = (c + d) % 4
        cols = pl.ds(pl.multiple_of(share * to, share), share)
        zcopies.append(send(zc.at[:, cols], zb.at[mine, :], zs.at[d], zr.at[d], b, to))
    third = []
    for i in range(3):
        second[i].wait_recv()
        third.append(send(far[i], far[i], ws.at[2, i], wr.at[2, i], b, mate))
    for d in (2, 1, 3):
        to = (c + d) % 4
        cols = pl.ds(pl.multiple_of(share * to + share, share), share)
        acopies.append(send(ext.at[:, cols], ab.at[mine, :], as_.at[d], ar.at[d], b, to))
    zb[mine, :] = zc[:, pl.ds(pl.multiple_of(share * c, share), share)]
    ab[mine, :] = ext[:, pl.ds(pl.multiple_of(share * c + share, share), share)]
    for copy in first + third:
        copy.wait()
    for copy in second:
        copy.wait_send()
    for copy in zcopies:
        copy.wait()
    fcopies = []
    width = 512
    per = width // PTS
    for n in range(share // width):
        cols = slice(n * width, (n + 1) * width)
        zcol = zb[:, cols]
        total = None
        for i in range(4):
            u = tn(w1[i], zcol)
            h = (u * sigmoid(u)).astype(BF16)
            part = tn(w2[i], h)
            total = part if total is None else total + part
        if n == 0:
            for copy in acopies:
                copy.wait()
        acol = (ab[:, cols].astype(F32) + total).astype(BF16)
        al[:, cols] = acol
        fx[n * per : (n + 1) * per] = tn(acol, wf[...]).astype(BF16).reshape(per, PTS, PTS)
        for d in (2, 1, 3):
            to = (c + d) % 4
            part = pl.ds(pl.multiple_of(quarter * to, quarter), quarter)
            fcopies.append(
                send(
                    fx.at[n * per : (n + 1) * per, part, :],
                    fp.at[pl.ds(c * (share // PTS) + n * per, per)],
                    fs.at[n, d], fr.at[n, d], b, to,
                )
            )
    part = pl.ds(pl.multiple_of(quarter * c, quarter), quarter)
    fp[pl.ds(c * (share // PTS), share // PTS)] = fx[:, part, :]
    for copy in fcopies:
        copy.wait()


def ocean_kernel(
    inv, slot, fp, mask, ct, wo_one, wo_two, state_all, cot_all,
    dstate, dfp, ctb, go1, go2,
    cts, fm, sp, rf, bk, rb, st, ctv, wa, wb, perm,
    lsem, cs, cr, ws, wr, ss, sr, rs, rr,
):
    b, c, mate, across, diag = place()
    bands = lax.axis_size("band")
    q, z = b // ZLEN, b % ZLEN
    groups = bands // ZLEN
    quarter = st.shape[0]
    blocks = fp.shape[0]
    rows, points = ct.shape
    share = ctb.shape[1]

    def greet(i, _):
        signal((b + i) % bands, c)
        return 0

    lax.fori_loop(1, bands, greet, 0)
    for d in (1, 2, 3):
        signal(b, (c + d) % 4)
    loads = []
    for i, (src, dst) in enumerate(((state_all, st), (cot_all, ctv))):
        loads.append(
            pltpu.make_async_copy(
                src.at[pl.ds(pl.multiple_of(quarter * c, quarter), quarter), 0], dst, lsem.at[i]
            )
        )
        loads[-1].start()
    fm[:blocks] = fp[...] * mask[...]
    fm[blocks] = jnp.zeros(fm.shape[1:], BF16)

    def pack(s, _):
        sp[s] = fm[inv[s]]
        return 0

    lax.fori_loop(0, 2 * bands, pack, 0)
    pl.semaphore_wait(pltpu.get_barrier_semaphore(), bands - 1 + 3)

    def couple(i, _):
        d = i // ZLEN
        to = ((q + d) % groups) * ZLEN + (z + i % ZLEN) % ZLEN
        send(sp.at[pl.ds(2 * to, 2)], rf.at[pl.ds(2 * b, 2)], ss, sr.at[d], to, c)
        return 0

    lax.fori_loop(1, bands, couple, 0)
    wide = wo_one.shape[1]
    mine_wide = pl.ds(pl.multiple_of(c * wide, wide), wide)
    mine = pl.ds(pl.multiple_of(c * rows, rows), rows)
    copies, late = [], []
    cts[:, :points] = ct[...]
    cts[:, points:] = jnp.zeros((rows, cts.shape[1] - points), BF16)
    for d in (2, 1, 3):
        to = (c + d) % 4
        copies.append(send(wo_one, wa.at[:, mine_wide], ws.at[0, d], wr.at[0, d], b, to))
        copies.append(send(wo_two, wb.at[mine_wide, :], ws.at[1, d], wr.at[1, d], b, to))
    for d in (2, 1, 3):
        to = (c + d) % 4
        cols = pl.ds(pl.multiple_of(share * to, share), share)
        late.append(send(cts.at[:, cols], ctb.at[mine, :], cs.at[d], cr.at[d], b, to))
    wa[:, mine_wide] = wo_one[...]
    wb[mine_wide, :] = wo_two[...]
    ctb[mine, :] = cts[:, pl.ds(pl.multiple_of(share * c, share), share)]
    rf[pl.ds(2 * b, 2)] = sp[pl.ds(2 * b, 2)]
    span = 2 * ZLEN
    size = span * quarter
    r = lax.broadcasted_iota(jnp.int32, (size, size), 0)
    k = lax.broadcasted_iota(jnp.int32, (size, size), 1)
    perm[...] = jnp.where((r % span) * quarter + r // span == k, 1.0, 0.0).astype(BF16)
    go1[...] = jnp.zeros(go1.shape, F32)
    go2[...] = jnp.zeros(go2.shape, F32)
    for load in loads:
        load.wait()
    for copy in copies:
        copy.wait()
    drain(rf.at[pl.ds(0, span - 2)], sr.at[0])

    def step(d, _):
        @pl.when(d > 0)
        def _():
            drain(rf.at[pl.ds(0, span)], sr.at[d])

        src = (q + groups - d) % groups
        at = pl.ds(pl.multiple_of(src * span, span), span)
        force = nn(perm[...], rf[at].reshape(size, PTS)).astype(BF16)
        both = jnp.concatenate([st[:, at, :].reshape(size, PTS), force], axis=1)
        cot = ctv[:, at, :].reshape(size, PTS)
        pre = nn(both, wa[...])
        sig = sigmoid(pre)
        act = pre * sig
        grad = (nt(cot, wb[...]) * (sig + act * (1.0 - sig))).astype(BF16)
        go2[...] += tn(cot, act.astype(BF16))
        go1[...] += tn(both, grad)
        back = nt(grad, wa[...])
        dstate[:, at, :] = (
            (cot.astype(F32) + back[:, :PTS]).astype(BF16).reshape(quarter, span, PTS)
        )
        bk[at] = tn(perm[...], back[:, PTS:].astype(BF16)).astype(BF16).reshape(span, quarter, PTS)

        def give(i, _):
            @pl.when(d + i > 0)
            def _():
                to = src * ZLEN + (z + i) % ZLEN
                send(bk.at[pl.ds(2 * to, 2)], rb.at[pl.ds(2 * b, 2)], rs, rr, to, c)

            return 0

        lax.fori_loop(0, ZLEN, give, 0)
        return 0

    lax.fori_loop(0, groups, step, 0)
    rb[pl.ds(2 * b, 2)] = bk[pl.ds(2 * b, 2)]
    drain(sp.at[pl.ds(0, 2 * bands - 2)], ss)
    drain(bk.at[pl.ds(0, 2 * bands - 2)], rs)
    drain(rb.at[pl.ds(0, 2 * bands - 2)], rr)

    def unpack(k, _):
        dfp[k] = rb[slot[k]] * mask[k]
        return 0

    lax.fori_loop(0, blocks, unpack, 0)
    for copy in late:
        copy.wait()


def backward_kernel(
    dfp, zb, al, ctb, w1, w2, wf, ext, taps,
    datmos, gw1, gw2, gwf, gk,
    dfb, hid, slope, gb, gc, dzb, dzc, dext,
    ds_, dr, gs, gr, zs, zr, hs, hr,
):
    b, c, mate, across, diag = place()
    bands = lax.axis_size("band")
    up, down = (b + bands - 1) % bands, (b + 1) % bands
    rows, points = datmos.shape
    share = zb.shape[1]
    own_blocks = share // PTS
    quarter = dfp.shape[1]
    signal(up, c)
    signal(down, c)
    for d in (1, 2, 3):
        signal(b, (c + d) % 4)
    pl.semaphore_wait(pltpu.get_barrier_semaphore(), 5)
    part = pl.ds(pl.multiple_of(quarter * c, quarter), quarter)
    dcopies = []
    for d in (2, 1, 3):
        to = (c + d) % 4
        dcopies.append(
            send(
                dfp.at[pl.ds(own_blocks * to, own_blocks)], dfb.at[:, part, :],
                ds_.at[d], dr.at[d], b, to,
            )
        )
    dfb[:, part, :] = dfp[pl.ds(own_blocks * c, own_blocks)]
    width = 512
    for n in range(share // width):
        cols = slice(n * width, (n + 1) * width)
        for i in range(4):
            u = tn(w1[i], zb[:, cols])
            sig = sigmoid(u)
            act = u * sig
            hid[i, :, cols] = act.astype(BF16)
            slope[i, :, cols] = sig + act * (1.0 - sig)
    for copy in dcopies:
        copy.wait()
    flux = dfb[...].reshape(share, PTS)
    gwf[...] = nn(al[...], flux)
    gb[...] = (ctb[...].astype(F32) + nt(wf[...], flux)).astype(BF16)
    gcopies, zcopies = [], []
    lanes = pl.ds(pl.multiple_of(share * c, share), share)
    for d in (2, 1, 3):
        to = (c + d) % 4
        theirs = pl.ds(pl.multiple_of(rows * to, rows), rows)
        gcopies.append(send(gb.at[theirs, :], gc.at[:, lanes], gs.at[d], gr.at[d], b, to))
    mine = pl.ds(pl.multiple_of(rows * c, rows), rows)
    gc[:, lanes] = gb[mine, :]
    for n in range(share // width):
        cols = slice(n * width, (n + 1) * width)
        gcol = gb[:, cols]
        zcol = zb[:, cols]
        total = None
        for i in range(4):
            du = (nn(w2[i], gcol) * slope[i, :, cols]).astype(BF16)
            g2 = nt(hid[i, :, cols], gcol)
            g1 = nt(zcol, du)
            gw2[i] = g2 if n == 0 else gw2[i] + g2
            gw1[i] = g1 if n == 0 else gw1[i] + g1
            piece = nn(w1[i], du)
            total = piece if total is None else total + piece
        dzb[:, cols] = total.astype(BF16)
        for d in (2, 1, 3):
            to = (c + d) % 4
            theirs = pl.ds(pl.multiple_of(rows * to, rows), rows)
            at = pl.ds(pl.multiple_of(share * c + n * width, width), width)
            zcopies.append(
                send(dzb.at[theirs, cols], dzc.at[:, at], zs.at[n, d], zr.at[n, d], b, to)
            )
    dzc[:, lanes] = dzb[mine, :]
    for copy in zcopies:
        copy.wait()
    halo = [
        send(dzc.at[:, points - share : points], dext.at[:, :share], hs.at[0], hr.at[0], down, c),
        send(dzc.at[:, :share], dext.at[:, share + points :], hs.at[1], hr.at[1], up, c),
    ]
    dext[:, share : share + points] = dzc[:, :points]
    width = 384
    low = share - LON
    high = share + LON
    sums = [jnp.zeros((rows, 128), F32) for _ in range(3)]
    for at in range(0, points, width):
        grad = dzc[:, at : at + width].astype(F32)
        views = (
            shifted(ext, at + low // 128 * 128, low % 128, width),
            ext[:, at + share : at + share + width].astype(F32),
            shifted(ext, at + high // 128 * 128, high % 128, width),
        )
        for i in range(3):
            prod = views[i] * grad
            for o in range(0, width, 128):
                sums[i] = sums[i] + prod[:, o : o + 128]
    lane = lax.broadcasted_iota(jnp.int32, (rows, 128), 1)
    whole = [jnp.sum(s, axis=1, keepdims=True) for s in sums]
    gk[...] = jnp.where(
        lane == 0, whole[0], jnp.where(lane == 1, whole[1], jnp.where(lane == 2, whole[2], 0.0))
    )
    for copy in gcopies:
        copy.wait()
    for copy in halo:
        copy.wait()

    @pl.when(b == 0)
    def _():
        dext[:, :share] = jnp.zeros((rows, share), BF16)

    @pl.when(b == bands - 1)
    def _():
        dext[:, share + points :] = jnp.zeros((rows, share), BF16)

    t0, t1, t2 = taps[:, 0:1], taps[:, 1:2], taps[:, 2:3]
    for at in range(0, points, width):
        datmos[:, at : at + width] = (
            gc[:, at : at + width].astype(F32)
            + t0 * shifted(dext, at + high // 128 * 128, high % 128, width)
            + t1 * dext[:, at + share : at + share + width].astype(F32)
            + t2 * shifted(dext, at + low // 128 * 128, low % 128, width)
        ).astype(BF16)


def reduce_kernel(
    gw1, gw2, gwf, gk, go1, go2,
    dw1, dw2, dwf, dk, do1, do2,
    gs, ra, rx, hx, own, t, r1, fs, r2, fr, ag, tb, out,
    s0, q0, s1, q1, s2, q2, s3, q3, s4, q4,
):
    b, c, mate, across, diag = place()
    bands = lax.axis_size("band")
    q, z = b // ZLEN, b % ZLEN
    groups = bands // ZLEN
    for d in (1, 2, 3):
        signal(b, (c + d) % 4)
    for d in range(1, groups):
        signal(((q + d) % groups) * ZLEN + z, c)
    for d in range(1, ZLEN):
        signal(q * ZLEN + (z + d) % ZLEN, c)
    for i in range(4):
        for j in range(2):
            gs[i, j * 256 : j * 256 + 256] = gw1[i, :, j * 128 : j * 128 + 128].astype(BF16)
            gs[i, 512 + j * 256 : 768 + j * 256] = gw2[i, :, j * 128 : j * 128 + 128].astype(BF16)
        gs[i, 1024:1280] = go1[:, i * 128 : i * 128 + 128].astype(BF16)
        gs[i, 1280:1408] = go2[:, i * 128 : i * 128 + 128].astype(BF16)
        gs[i, 1408:1472] = gwf[i * 64 : i * 64 + 64, :].astype(BF16)
        gs[i, 1472:1536] = jnp.zeros((64, 128), BF16)
    gs[c, 1472:1536] = gk[...].astype(BF16)
    pl.semaphore_wait(pltpu.get_barrier_semaphore(), 3 + groups - 1 + ZLEN - 1)
    ca = send(gs.at[diag], ra.at[1], s0.at[1], q0.at[1], b, mate)
    cb = send(gs.at[mate], ra.at[0], s0.at[0], q0.at[0], b, mate)
    ca.wait()
    hx[...] = (gs[across].astype(F32) + ra[1].astype(F32)).astype(BF16)
    cc = send(hx, rx, s0.at[2], q0.at[2], b, across)
    cb.wait()
    own[...] = gs[c].astype(F32) + ra[0].astype(F32)
    cc.wait()
    size = t.shape[1]
    for i in range(groups):
        rows = slice(i * size, (i + 1) * size)
        t[i] = (own[rows] + rx[rows].astype(F32)).astype(BF16)
    copies = []
    for d in range(1, groups):
        to = (q + d) % groups
        copies.append(send(t.at[to], r1.at[q], s1.at[d], q1.at[d], to * ZLEN + z, c))
    r1[q] = t[q]
    for copy in copies:
        copy.wait()
    total = r1[0].astype(F32)
    for i in range(1, groups):
        total = total + r1[i].astype(F32)
    fs[...] = total.reshape(fs.shape)
    copies = []
    for d in range(1, ZLEN):
        to = (z + d) % ZLEN
        copies.append(send(fs.at[to], r2.at[z], s2.at[d], q2.at[d], q * ZLEN + to, c))
    r2[z] = fs[z]
    for copy in copies:
        copy.wait()
    total = r2[0]
    for i in range(1, ZLEN):
        total = total + r2[i]
    fr[...] = total
    copies = []
    for d in range(1, ZLEN):
        to = (z + d) % ZLEN
        copies.append(send(fr, ag.at[z], s3.at[d], q3.at[d], q * ZLEN + to, c))
    ag[z] = total
    for copy in copies:
        copy.wait()
    tb[...] = ag[...].reshape(size, 128).astype(BF16)
    copies = []
    for d in range(1, groups):
        to = (q + d) % groups
        copies.append(send(tb, out.at[q], s4.at[d], q4.at[d], to * ZLEN + z, c))
    out[q] = tb[...]
    for copy in copies:
        copy.wait()
    flat = out[...].reshape(groups * size, 128).astype(F32)
    for j in range(2):
        dw1[:, j * 128 : j * 128 + 128] = flat[j * 256 : j * 256 + 256]
        dw2[:, j * 128 : j * 128 + 128] = flat[512 + j * 256 : 768 + j * 256]
    do1[...] = flat[1024:1280]
    do2[...] = flat[1280:1408].T
    dwf[...] = flat[1408:1472]
    dk[...] = flat[1472:1536]


def call(body, ident, outs, scratch, args, specs):
    return pl.pallas_call(
        body,
        out_shape=[jax.ShapeDtypeStruct(s, t) for s, t in outs],
        in_specs=specs,
        out_specs=[pl.BlockSpec(memory_space=VMEM)] * len(outs),
        scratch_shapes=scratch,
        compiler_params=pltpu.CompilerParams(
            collective_id=ident, has_side_effects=True, vmem_limit_bytes=LIMIT
        ),
    )(*args)


def local(
    atmos, kernels, w_one, w_two, w_flux, sea_mask, route,
    ocean_state, ct_atmos, ct_ocean, wo_one, wo_two,
):
    c = lax.axis_index("chan")
    chans = lax.axis_size("chan")
    bands = lax.axis_size("band")
    rows, points = atmos.shape
    blocks = points // PTS
    own_blocks = -(-blocks // chans)
    share = own_blocks * PTS
    padded = own_blocks * chans
    quarter = PTS // chans
    slots = ocean_state.shape[2]
    hid = w_one.shape[2]
    full = rows * chans
    whole = hid * chans
    wide = wo_one.shape[1]
    total = wide * chans
    vm = pl.BlockSpec(memory_space=VMEM)
    sm = pl.BlockSpec(memory_space=pltpu.SMEM)
    anywhere = pl.BlockSpec(memory_space=pl.ANY)

    target = route[:, 0]
    order = jnp.arange(blocks, dtype=jnp.int32)
    earlier = (target[None, :] == target[:, None]) & (order[None, :] < order[:, None])
    slot_of = target * (slots // bands) + jnp.sum(earlier.astype(jnp.int32), axis=1)
    hit = slot_of[:, None] == jnp.arange(slots, dtype=jnp.int32)[None, :]
    inv = padded + jnp.sum(jnp.where(hit, order[:, None] - padded, 0), axis=0)
    slot_of = jnp.pad(slot_of, (0, padded - blocks))
    mask = lax.dynamic_slice_in_dim(sea_mask.reshape(blocks, PTS), c * quarter, quarter, 1)
    mask = jnp.pad(mask.astype(BF16), ((0, padded - blocks), (0, 0)))
    mask = jnp.broadcast_to(mask[:, :, None], (padded, quarter, PTS))
    taps = kernels[0].T

    ext, zb, al, w1, w2, wf, fp = call(
        forward_kernel, 0,
        [
            ((rows, points + 2 * share), BF16),
            ((full, share), BF16),
            ((full, share), BF16),
            ((chans, full, hid), BF16),
            ((chans, hid, full), BF16),
            ((full, PTS), BF16),
            ((padded, quarter, PTS), BF16),
        ],
        [
            VMEM((rows, padded * PTS), BF16),
            VMEM((full, share), BF16),
            VMEM((own_blocks, PTS, PTS), BF16),
            DMA((2,)), DMA((2,)), DMA((3, 3)), DMA((3, 3)), DMA((4,)), DMA((4,)),
            DMA((4,)), DMA((4,)), DMA((3, 4)), DMA((3, 4)),
        ],
        (atmos, taps, w_one[0], w_two[0], w_flux),
        [vm] * 5,
    )
    dstate, dfp, ctb, go1, go2 = call(
        ocean_kernel, 1,
        [
            ((quarter, slots, PTS), BF16),
            ((padded, quarter, PTS), BF16),
            ((full, share), BF16),
            ((2 * PTS, total), F32),
            ((PTS, total), F32),
        ],
        [
            VMEM((rows, padded * PTS), BF16),
            VMEM((padded + 1, quarter, PTS), BF16),
            VMEM((slots, quarter, PTS), BF16),
            VMEM((slots, quarter, PTS), BF16),
            VMEM((slots, quarter, PTS), BF16),
            VMEM((slots, quarter, PTS), BF16),
            VMEM((quarter, slots, PTS), BF16),
            VMEM((quarter, slots, PTS), BF16),
            VMEM((2 * PTS, total), BF16),
            VMEM((total, PTS), BF16),
            VMEM((2 * ZLEN * quarter, 2 * ZLEN * quarter), BF16),
            DMA((2,)), DMA((4,)), DMA((4,)), DMA((2, 4)), DMA((2, 4)),
            DMA, DMA((bands // ZLEN,)), DMA, DMA,
        ],
        (inv, slot_of, fp, mask, ct_atmos, wo_one, wo_two, ocean_state, ct_ocean),
        [sm, sm, vm, vm, vm, vm, vm, anywhere, anywhere],
    )
    datmos, gw1, gw2, gwf, gk = call(
        backward_kernel, 2,
        [
            ((rows, points), BF16),
            ((chans, full, hid), F32),
            ((chans, hid, full), F32),
            ((full, PTS), F32),
            ((rows, 128), F32),
        ],
        [
            VMEM((own_blocks, PTS, PTS), BF16),
            VMEM((chans, hid, share), BF16),
            VMEM((chans, hid, share), F32),
            VMEM((full, share), BF16),
            VMEM((rows, padded * PTS), BF16),
            VMEM((full, share), BF16),
            VMEM((rows, padded * PTS), BF16),
            VMEM((rows, points + 2 * share), BF16),
            DMA((4,)), DMA((4,)), DMA((4,)), DMA((4,)), DMA((3, 4)), DMA((3, 4)),
            DMA((2,)), DMA((2,)),
        ],
        (dfp, zb, al, ctb, w1, w2, wf, ext, taps),
        [vm] * 9,
    )
    groups = bands // ZLEN
    flat = 1536
    size = flat // groups
    small = size // ZLEN
    dw1, dw2, dwf, dk, do1, do2 = call(
        reduce_kernel, 3,
        [
            ((full, hid), F32),
            ((hid, full), F32),
            ((rows, PTS), F32),
            ((rows, 128), F32),
            ((2 * PTS, wide), F32),
            ((wide, PTS), F32),
        ],
        [
            VMEM((4, flat, 128), BF16),
            VMEM((2, flat, 128), BF16),
            VMEM((flat, 128), BF16),
            VMEM((flat, 128), BF16),
            VMEM((flat, 128), F32),
            VMEM((groups, size, 128), BF16),
            VMEM((groups, size, 128), BF16),
            VMEM((ZLEN, small, 128), F32),
            VMEM((ZLEN, small, 128), F32),
            VMEM((small, 128), F32),
            VMEM((ZLEN, small, 128), F32),
            VMEM((size, 128), BF16),
            VMEM((groups, size, 128), BF16),
            DMA((3,)), DMA((3,)), DMA((groups,)), DMA((groups,)), DMA((ZLEN,)), DMA((ZLEN,)),
            DMA((ZLEN,)), DMA((ZLEN,)), DMA((groups,)), DMA((groups,)),
        ],
        (gw1, gw2, gwf, gk, go1, go2),
        [vm] * 6,
    )
    return (
        datmos, dk[:, :3].T[None], dw1[None], dw2[None], dwf, dstate[:, None], do1, do2,
    )


def solution(mesh):
    in_specs = (
        P("chan", "band"),
        P(None, None, "chan"),
        P(None, None, "chan"),
        P(None, "chan", None),
        P("chan", None),
        P("band"),
        P("band", None),
        P(None, "band", None, None),
        P("chan", "band"),
        P(None, "band", None, None),
        P(None, "chan"),
        P("chan", None),
    )
    out_specs = (
        P("chan", "band"),
        P(None, None, "chan"),
        P(None, None, "chan"),
        P(None, "chan", None),
        P("chan", None),
        P("chan", "band", None, None),
        P(None, "chan"),
        P("chan", None),
    )
    return jax.shard_map(local, mesh=mesh, in_specs=in_specs, out_specs=out_specs, check_vma=False)
```

time: 1260 us -> 209 us (0.17)
  waiting for transfers between devices: 713 us -> 0 us
  blocking collectives: 360 us -> 0 us
  Pallas kernels: 0 us -> 190 us
  matrix products: 63.9 us -> 0 us
  starting transfers between devices: 37.9 us -> 0 us
  local copies, waits for them, and re-layouts: 50.4 us -> 13.4 us
  between operations: 14.6 us -> 0.71 us
    psum x1 -> x0, blocking collectives: 360 us -> none  [local(): lax.psum((jnp.stack(tap_grads), jnp.stack(one_grads), jnp.stack(two_grads...]
    psum x2 -> x0, waiting for transfers between devices: 347 us -> none  [the longest x1 293 us: local(): lax.psum((jnp.stack(tap_grads), jnp.stack(one_grads), jnp.stack(two_grads...]
    pallas_call x0 -> x4, Pallas kernels: none -> 190 us  [call(): pl.pallas_call(body, out_shape=[jax.ShapeDtypeStruct(s, t) for s, t in ou...]
    reduce_scatter x4 -> x0, waiting for transfers between devices: 138 us -> none  [chan_share(): lax.psum_scatter(for_sending(terms), 'chan', scatter_dimension=0, tiled=T...]
    all_to_all x2 -> x0, waiting for transfers between devices: 122 us -> none  [couple(): lax.all_to_all(blocks, 'band', split_axis=1, concat_axis=1, tiled=True)]
    all_gather x3 -> x0, waiting for transfers between devices: 96.2 us -> none  [whole_chan(): return lax.all_gather(field, 'chan', axis=0, tiled=True)]
    dot_general x19 -> x0, matrix products: 63.9 us -> none  [the longest x14 55.7 us: contract(): lax.dot_general(left, right, (((left_dim,), (right_dim,)), ((), ())), pre...]
    all_to_all x2 -> x0, starting transfers between devices: 26.1 us -> none  [couple(): lax.all_to_all(blocks, 'band', split_axis=1, concat_axis=1, tiled=True)]
  transfers between devices with their start and end apart: 15 -> 0, of which waited for: 15 -> 0; matrix products, arithmetic and copies ran while one was open for 4% -> 0% of each run, Pallas kernels for 0% -> 0%
where the time goes in v1:
time: 209 us; the launch traced here: 207 us
  Pallas kernels  190 us (91%)
  local copies, waits for them, and re-layouts  13.4 us (6%)
  other arithmetic  3.66 us (2%)
    pallas_call x4, Pallas kernels, call(): pl.pallas_call(body, out_shape=[jax.ShapeDtypeStruct(s, t) for s, t in ou...  190 us
    unnamed x15, local copies, waits for them, and re-layouts  11 us

profile of v1, /device:TPU:8, one launch (start us, length us, event | category | flops | bytes accessed | tf_op | source)
XLA Modules:
  0.0 207.4 jit_solution(8221844565182592331)
XLA Ops:
  0.6 0.9 convert_reduce_fusion
  1.5 0.7 multiply_add_fusion
  2.2 0.7 fusion.1
  2.9 0.5 pad.8.slot
  3.4 0.1 select_reduce_fusion
  3.5 0.5 broadcast_add_fusion.inv
  4.0 0.8 dynamic-slice_convert_fusion
  4.8 1.4 copy.23
  6.2 1.0 broadcast_in_dim.37.mask
  7.2 44.5 %shard_map.179 = (bf16[64,8832]{1,0:T(8,128)(2,1)}, bf16[256,1536]{1,0:T(8,128)(2,1)}, bf16[256,1536]{1,0:T(8,128)(2,1)}, bf16[4,256,256]{2,1,0:T(8,128)(2,1)}, ...) custom-call(bf16[64,5760]{1,0:T(8,128)(2,1)} %atmos.1, f32[64,3]{1,0:T(8,128)} %bitcast.24, ...), custom_call_target="tpu_custom_call" | custom-call | tf_op jit(solution)/shard_map/pallas_call | solution.py:518
  51.7 62.1 %shard_map.180 = (bf16[32,128,128]{2,1,0:T(8,128)(2,1)}, bf16[48,32,128]{2,1,0:T(8,128)(2,1)}, bf16[256,1536]{1,0:T(8,128)(2,1)}, f32[256,512]{1,0:T(8,128)}, f32[128,512]{1,0:T(8,128)}) custom-call(s32[128]{0:T(128)} %broadcast_add_fusion.inv, s32[48]{0:T(128)} %pad.8.slot, bf16[48,32,128]{2,1,0:T(8,128)(2,1)} %get-tuple-element.31.fp, ...), custom_call_target="tpu_custom_call" | custom-call | tf_op jit(solution)/shard_map/pallas_call | solution.py:518
  113.9 0.0 copy-start
  113.9 41.1 %shard_map.181 = (bf16[64,5760]{1,0:T(8,128)(2,1)}, f32[4,256,256]{2,1,0:T(8,128)}, f32[4,256,256]{2,1,0:T(8,128)}, f32[256,128]{1,0:T(8,128)}, f32[64,128]{1,0:T(8,128)}) custom-call(bf16[48,32,128]{2,1,0:T(8,128)(2,1)} %get-tuple-element.32.dfp, bf16[256,1536]{1,0:T(8,128)(2,1)} %get-tuple-element.33.zb, bf16[256,1536]{1,0:T(8,128)(2,1)} %get-tuple-element.34.al, ...), custom_call_target="tpu_custom_call" | custom-call | tf_op jit(solution)/shard_map/pallas_call | solution.py:518
  155.0 41.9 %shard_map.182 = (f32[256,256]{1,0:T(8,128)}, f32[256,256]{1,0:T(8,128)}, f32[64,128]{1,0:T(8,128)}, f32[64,128]{1,0:T(8,128)}, f32[256,128]{1,0:T(8,128)}, /*index=5*/f32[128,128]{1,0:T(8,128)}) custom-call(f32[4,256,256]{2,1,0:T(8,128)} %get-tuple-element.41.gw1, f32[4,256,256]{2,1,0:T(8,128)} %get-tuple-element.42.gw2, f32[256,128]{1,0:T(8,128)} %get-tuple-element.43.gwf, ...), custom_call_target="tpu_custom_call" | custom-call | tf_op jit(solution)/shard_map/pallas_call | solution.py:518
  196.9 0.0 copy-start.1
  196.9 0.0 copy-start.2
  196.9 0.8 slice_bitcast_fusion
  197.7 0.6 copy.24
  198.3 2.0 copy.33
  200.4 1.7 copy.34
  202.0 1.7 copy.35
  203.7 1.4 copy.36
  205.1 0.0 copy-done
  205.1 1.0 copy.37
  206.1 0.0 copy-done.1
  206.1 0.7 copy.38
  206.7 0.0 copy-done.2
  206.7 0.6 copy.39
  (2 shorter events, 0.0 us)
Async XLA Ops:
  113.9 91.2 %copy-start = (bf16[32,128,128]{2,1,0:T(8,128)(2,1)S(1)}, bf16[32,128,128]{2,1,0:T(8,128)(2,1)}, u32[]{:S(2)}) copy-start(bf16[32,128,128]{2,1,0:T(8,128)(2,1)} %get-tuple-element.51) | copy-start | bytes 3145732
  196.9 9.2 %copy-start.1 = (f32[256,128]{1,0:T(8,128)S(1)}, f32[256,128]{1,0:T(8,128)}, u32[]{:S(2)}) copy-start(f32[256,128]{1,0:T(8,128)} %get-tuple-element.84) | copy-start | bytes 393220
  196.9 9.8 %copy-start.2 = (f32[128,128]{1,0:T(8,128)S(1)}, f32[128,128]{1,0:T(8,128)}, u32[]{:S(2)}) copy-start(f32[128,128]{1,0:T(8,128)} %get-tuple-element.85) | copy-start | bytes 196612

commit v2 on v0

v2 whole, which is shorter than its diff:
```python
import functools

import jax
import jax.numpy as jnp
from jax import lax
from jax.experimental import pallas as pl
from jax.experimental.pallas import tpu as pltpu
from jax.sharding import PartitionSpec as P

PTS = 128
LON = 1440
MESH = pl.DeviceIdType.MESH
F32 = jnp.float32
BF16 = jnp.bfloat16
VMEM = pltpu.VMEM
DMA = pltpu.SemaphoreType.DMA
ZLEN = 8
LIMIT = 56 * 1024 * 1024


def nn(a, b):
    return lax.dot_general(a, b, (((1,), (0,)), ((), ())), preferred_element_type=F32)


def tn(a, b):
    return lax.dot_general(a, b, (((0,), (0,)), ((), ())), preferred_element_type=F32)


def nt(a, b):
    return lax.dot_general(a, b, (((1,), (1,)), ((), ())), preferred_element_type=F32)


def sigmoid(v):
    return 0.5 * jnp.tanh(0.5 * v) + 0.5


def place():
    b, c = lax.axis_index("band"), lax.axis_index("chan")
    mate = (c // 2) * 2 + (1 - c % 2)
    return b, c, mate, (c + 2) % 4, (mate + 2) % 4


def send(src, dst, ssem, rsem, b, c):
    copy = pltpu.make_async_remote_copy(
        src_ref=src,
        dst_ref=dst,
        send_sem=ssem,
        recv_sem=rsem,
        device_id=(b, c),
        device_id_type=MESH,
    )
    copy.start()
    return copy


def drain(ref, sem):
    pltpu.make_async_copy(ref, ref, sem).wait()


def signal(b, c):
    pl.semaphore_signal(
        pltpu.get_barrier_semaphore(), inc=1, device_id=(b, c), device_id_type=MESH
    )


def shifted(ref, start, extra, width):
    wide = ref[:, start : start + width + 128].astype(F32)
    return pltpu.roll(wide, width + 128 - extra, axis=1)[:, :width]


def table_kernel(route, table):
    blocks = route.shape[0]
    col = route[...]
    k = lax.broadcasted_iota(jnp.int32, (blocks, blocks), 0)
    j = lax.broadcasted_iota(jnp.int32, (blocks, blocks), 1)
    row = jnp.sum(jnp.where(k == j, col, 0), axis=0, keepdims=True)
    rank = jnp.sum(jnp.where((row == col) & (j < k), 1, 0), axis=1, keepdims=True)
    slot = col * 2 + rank
    k = lax.broadcasted_iota(jnp.int32, (blocks, 128), 0)
    s = lax.broadcasted_iota(jnp.int32, (blocks, 128), 1)
    empty = 48
    inv = empty + jnp.sum(jnp.where(slot == s, k - empty, 0), axis=0, keepdims=True)
    back = jnp.sum(jnp.where(k == s, slot, 0), axis=0, keepdims=True)
    line = lax.broadcasted_iota(jnp.int32, (8, 128), 0)
    table[...] = jnp.where(line == 0, inv, back)


def finish_kernel(dat, dst, out, gk, datmos, dk, dw1, dw2, dwf, dstate, do1, do2):
    datmos[...] = dat[...]
    dstate[...] = dst[...]
    for j in range(2):
        dw1[:, j * 128 : j * 128 + 128] = out[j * 256 : j * 256 + 256].astype(F32)
        dw2[:, j * 128 : j * 128 + 128] = out[512 + j * 256 : 768 + j * 256].astype(F32)
    dwf[...] = out[1024:1088].astype(F32)
    do1[...] = out[1152:1408].astype(F32)
    do2[...] = out[1408:1536].astype(F32).T
    dk[...] = gk[:3, :64]


def main_kernel(
    table, atmos, taps, w_one, w_two, w_flux, sea, wo_one, wo_two, ct_all, state_all, cot_all,
    dat, dst, out, gkout,
    ext, a0, zc, zb, ab, alm, w1, w2, wf, fx, fm, mk, hid, slope,
    cts, ctb, sp, rf, bk, rb, st, ctv, ds, wa, wb, perm, go1, go2,
    dfp, dfb, gb, gc, dzb, dzc, dext, dzacc, dubuf, gwf,
    gs, ra, hx, rx, gso, rao, hxo, rxo, own, owno, t, r1, fs, r2, fr, ag, tb, gkt, gkr,
    lsem, hs, hr, ws, wr, as_, ar, zs, zr, fxs, fxr, cs, cr, ss, sr, rs, rr,
    os_, or_, dfs, dfr, gsd, grd, dzs, dzr, h2s, h2r, s0, q0, s1, q1, s2, q2, s3, q3, s4, q4, ks, kr,
):
    b, c, mate, across, diag = place()
    bands = lax.axis_size("band")
    up, down = (b + bands - 1) % bands, (b + 1) % bands
    q, z = b // ZLEN, b % ZLEN
    groups = bands // ZLEN
    flip = ((q // 2) * 2 + (1 - q % 2)) * ZLEN + z
    rows, points = atmos.shape
    share = zb.shape[1]
    own_blocks = share // PTS
    quarter = st.shape[0]
    blocks = dfp.shape[0]
    wide = wo_one.shape[1]
    peers = [(c + 2) % 4, (c + 1) % 4, (c + 3) % 4]
    ds_of = (2, 1, 3)

    def greet(i, _):
        signal((b + i) % bands, c)
        return 0

    lax.fori_loop(1, bands, greet, 0)
    for d in (1, 2, 3):
        signal(b, (c + d) % 4)
    signal(flip, across)
    loads = [
        pltpu.make_async_copy(ct_all, cts.at[:, :points], lsem.at[0]),
        pltpu.make_async_copy(
            state_all.at[pl.ds(pl.multiple_of(quarter * c, quarter), quarter), 0], st, lsem.at[1]
        ),
        pltpu.make_async_copy(
            cot_all.at[pl.ds(pl.multiple_of(quarter * c, quarter), quarter), 0], ctv, lsem.at[2]
        ),
    ]
    for load in loads:
        load.start()
    mine = pl.ds(pl.multiple_of(c * rows, rows), rows)
    lanes = pl.ds(pl.multiple_of(share * c, share), share)
    part = pl.ds(pl.multiple_of(quarter * c, quarter), quarter)
    a0[:, :points] = atmos[...]
    a0[:, points:] = jnp.zeros((rows, a0.shape[1] - points), BF16)
    pl.semaphore_wait(pltpu.get_barrier_semaphore(), bands - 1 + 4)

    halo = [
        send(atmos.at[:, points - share :], ext.at[:, :share], hs.at[0], hr.at[0], down, c),
        send(atmos.at[:, :share], ext.at[:, share + points :], hs.at[1], hr.at[1], up, c),
    ]
    acopies = []
    for d, to in zip(ds_of, peers):
        cols = pl.ds(pl.multiple_of(share * to, share), share)
        acopies.append(send(a0.at[:, cols], ab.at[mine, :], as_.at[d], ar.at[d], b, to))
    mine_wide = pl.ds(pl.multiple_of(c * wide, wide), wide)
    theirs = pl.ds(pl.multiple_of(across * rows, rows), rows)
    theirs_wide = pl.ds(pl.multiple_of(across * wide, wide), wide)
    sources = (w_one, w_two, w_flux, wo_one, wo_two)
    near = (w1.at[c], w2.at[c], wf.at[mine, :], wa.at[:, mine_wide], wb.at[mine_wide, :])
    far = (
        w1.at[across], w2.at[across], wf.at[theirs, :],
        wa.at[:, theirs_wide], wb.at[theirs_wide, :],
    )
    first, second, third = [], [], []
    for i in range(5):
        second.append(send(sources[i], near[i], ws.at[1, i], wr.at[1, i], flip, across))
        first.append(send(sources[i], near[i], ws.at[0, i], wr.at[0, i], b, mate))
    w1[c] = w_one[...]
    w2[c] = w_two[...]
    wf[mine, :] = w_flux[...]
    wa[:, mine_wide] = wo_one[...]
    wb[mine_wide, :] = wo_two[...]
    ext[:, share : share + points] = atmos[...]
    zc[:, points:] = jnp.zeros((rows, zc.shape[1] - points), BF16)
    cts[:, points:] = jnp.zeros((rows, cts.shape[1] - points), BF16)
    mk[:, :points] = sea[...].astype(F32)
    mk[:, points:] = jnp.zeros((1, mk.shape[1] - points), F32)
    ab[mine, :] = a0[:, lanes]
    eye = lax.broadcasted_iota(jnp.int32, (rows, rows), 0) == lax.broadcasted_iota(
        jnp.int32, (rows, rows), 1
    )
    t0, t1, t2 = [
        jnp.sum(jnp.where(eye, taps[i : i + 1, :], 0.0), axis=1, keepdims=True) for i in range(3)
    ]
    for copy in halo:
        copy.wait()

    @pl.when(b == 0)
    def _():
        ext[:, :share] = jnp.zeros((rows, share), BF16)

    @pl.when(b == bands - 1)
    def _():
        ext[:, share + points :] = jnp.zeros((rows, share), BF16)

    width = 384
    low = share - LON
    high = share + LON
    for at in range(0, points, width):
        zc[:, at : at + width] = (
            t0 * shifted(ext, at + low // 128 * 128, low % 128, width)
            + t1 * ext[:, at + share : at + share + width].astype(F32)
            + t2 * shifted(ext, at + high // 128 * 128, high % 128, width)
        ).astype(BF16)
    width = 512
    steps = share // width
    per = width // PTS
    zcopies = []
    for n in range(steps):
        for d, to in zip(ds_of, peers):
            cols = pl.ds(pl.multiple_of(share * to + n * width, width), width)
            zcopies.append(
                send(
                    zc.at[:, cols], zb.at[mine, n * width : (n + 1) * width],
                    zs.at[n, d], zr.at[n, d], b, to,
                )
            )
    zb[mine, :] = zc[:, lanes]
    for i in range(5):
        second[i].wait_recv()
        third.append(send(far[i], far[i], ws.at[2, i], wr.at[2, i], b, mate))
    for i in range(3):
        first[i].wait()
        second[i].wait_send()
        third[i].wait()
    own_mask = mk[:, lanes]
    fcopies = []
    for n in range(steps):
        cols = slice(n * width, (n + 1) * width)
        for copy in zcopies[3 * n : 3 * n + 3]:
            copy.wait()
        zcol = zb[:, cols]
        total = None
        for i in range(4):
            u = tn(w1[i], zcol)
            sig = sigmoid(u)
            act = u * sig
            h = act.astype(BF16)
            hid[i, :, cols] = h
            slope[i, :, cols] = (sig + act * (1.0 - sig)).astype(BF16)
            piece = tn(w2[i], h)
            total = piece if total is None else total + piece
        if n == 0:
            for copy in acopies:
                copy.wait()
        acol = (ab[:, cols].astype(F32) + total).astype(BF16)
        acol = (acol.astype(F32) * own_mask[:, cols]).astype(BF16)
        alm[:, cols] = acol
        fx[n * per : (n + 1) * per] = tn(acol, wf[...]).astype(BF16).reshape(per, PTS, PTS)
        for d, to in zip(ds_of, peers):
            piece = pl.ds(pl.multiple_of(quarter * to, quarter), quarter)
            fcopies.append(
                send(
                    fx.at[n * per : (n + 1) * per, piece, :],
                    fm.at[pl.ds(c * own_blocks + n * per, per)],
                    fxs.at[n, d], fxr.at[n, d], b, to,
                )
            )
    fm[pl.ds(c * own_blocks, own_blocks)] = fx[:, part, :]
    fm[blocks] = jnp.zeros(fm.shape[1:], BF16)
    span = 2 * ZLEN
    size = span * quarter
    r = lax.broadcasted_iota(jnp.int32, (size, size), 0)
    k = lax.broadcasted_iota(jnp.int32, (size, size), 1)
    perm[...] = jnp.where((r % span) * quarter + r // span == k, 1.0, 0.0).astype(BF16)
    go1[...] = jnp.zeros(go1.shape, F32)
    go2[...] = jnp.zeros(go2.shape, F32)
    for load in loads:
        load.wait()
    for i in range(3, 5):
        first[i].wait()
        second[i].wait_send()
        third[i].wait()
    for copy in fcopies:
        copy.wait()

    def pack(s, _):
        sp[s] = fm[table[0, s]]
        return 0

    lax.fori_loop(0, 2 * bands, pack, 0)

    def couple(i, _):
        d = i // ZLEN
        to = ((q + d) % groups) * ZLEN + (z + i % ZLEN) % ZLEN
        send(sp.at[pl.ds(2 * to, 2)], rf.at[pl.ds(2 * b, 2)], ss, sr.at[d], to, c)
        return 0

    lax.fori_loop(1, bands, couple, 0)
    ctcopies = []
    for d, to in zip(ds_of, peers):
        cols = pl.ds(pl.multiple_of(share * to, share), share)
        ctcopies.append(send(cts.at[:, cols], ctb.at[mine, :], cs.at[d], cr.at[d], b, to))
    ctb[mine, :] = cts[:, lanes]
    rf[pl.ds(2 * b, 2)] = sp[pl.ds(2 * b, 2)]
    drain(rf.at[pl.ds(0, span - 2)], sr.at[0])

    def step(d, _):
        @pl.when(d > 0)
        def _():
            drain(rf.at[pl.ds(0, span)], sr.at[d])

        src = (q + groups - d) % groups
        at = pl.ds(pl.multiple_of(src * span, span), span)
        force = nn(perm[...], rf[at].reshape(size, PTS)).astype(BF16)
        both = jnp.concatenate([st[:, at, :].reshape(size, PTS), force], axis=1)
        cot = ctv[:, at, :].reshape(size, PTS)
        pre = nn(both, wa[...])
        sig = sigmoid(pre)
        act = pre * sig
        grad = (nt(cot, wb[...]) * (sig + act * (1.0 - sig))).astype(BF16)
        back = nt(grad, wa[...])
        bk[at] = tn(perm[...], back[:, PTS:].astype(BF16)).astype(BF16).reshape(span, quarter, PTS)

        def give(i, _):
            @pl.when(d + i > 0)
            def _():
                to = src * ZLEN + (z + i) % ZLEN
                send(bk.at[pl.ds(2 * to, 2)], rb.at[pl.ds(2 * b, 2)], rs, rr, to, c)

            return 0

        lax.fori_loop(0, ZLEN, give, 0)
        ds[:, at, :] = (
            (cot.astype(F32) + back[:, :PTS]).astype(BF16).reshape(quarter, span, PTS)
        )
        go2[...] += tn(cot, act.astype(BF16))
        go1[...] += tn(both, grad)
        return 0

    lax.fori_loop(0, groups, step, 0)
    dstore = pltpu.make_async_copy(ds, dst, lsem.at[3])
    dstore.start()
    rb[pl.ds(2 * b, 2)] = bk[pl.ds(2 * b, 2)]
    for i in range(4):
        gso[i, :256] = go1[:, i * 128 : i * 128 + 128].astype(BF16)
        gso[i, 256:] = go2[:, i * 128 : i * 128 + 128].astype(BF16)
    ocopies = [
        send(gso.at[diag], rao.at[1], os_.at[1], or_.at[1], b, mate),
        send(gso.at[mate], rao.at[0], os_.at[0], or_.at[0], b, mate),
    ]
    for copy in ctcopies:
        copy.wait()
    drain(rb.at[pl.ds(0, 2 * bands - 2)], rr)

    def unpack(k, _):
        dfp[k] = rb[table[1, k]]
        return 0

    lax.fori_loop(0, blocks, unpack, 0)
    dcopies = []
    for d, to in zip(ds_of, peers):
        dcopies.append(
            send(
                dfp.at[pl.ds(own_blocks * to, own_blocks)], dfb.at[:, part, :],
                dfs.at[d], dfr.at[d], b, to,
            )
        )
    dfb[:, part, :] = dfp[pl.ds(own_blocks * c, own_blocks)]
    for copy in ocopies:
        copy.wait()
    hxo[...] = (gso[across].astype(F32) + rao[1].astype(F32)).astype(BF16)
    owno[...] = gso[c].astype(F32) + rao[0].astype(F32)
    ocopy = send(hxo, rxo, os_.at[2], or_.at[2], b, across)
    gs[:, 1088:] = jnp.zeros((4, 64, 128), BF16)
    for copy in dcopies:
        copy.wait()
    flux = dfb[...].reshape(share, PTS)
    gb[...] = (ctb[...].astype(F32) + nt(wf[...], flux) * own_mask).astype(BF16)
    gwf[...] = nn(alm[...], flux)
    wcopies = []
    for turn, i in enumerate((diag, mate, across, c)):
        for n in range(steps):
            cols = slice(n * width, (n + 1) * width)
            du = (nn(w2[i], gb[:, cols]) * slope[i, :, cols].astype(F32)).astype(BF16)
            dubuf[:, cols] = du
            piece = nn(w1[i], du)
            if turn == 0:
                dzacc[:, cols] = piece
            elif turn < 3:
                dzacc[:, cols] += piece
            else:
                dzb[:, cols] = (dzacc[:, cols] + piece).astype(BF16)
        g1 = nt(zb[...], dubuf[...])
        g2 = nt(hid[i], gb[...])
        for j in range(2):
            gs[i, j * 256 : j * 256 + 256] = g1[:, j * 128 : j * 128 + 128].astype(BF16)
            gs[i, 512 + j * 256 : 768 + j * 256] = g2[:, j * 128 : j * 128 + 128].astype(BF16)
        gs[i, 1024:1088] = gwf[pl.ds(pl.multiple_of(rows * i, rows), rows), :].astype(BF16)
        if turn == 0:
            wcopies.append(send(gs.at[diag], ra.at[1], s0.at[1], q0.at[1], b, mate))
        if turn == 1:
            wcopies.append(send(gs.at[mate], ra.at[0], s0.at[0], q0.at[0], b, mate))
        if turn == 2:
            wcopies[0].wait()
            hx[...] = (gs[across].astype(F32) + ra[1].astype(F32)).astype(BF16)
            wcopies.append(send(hx, rx, s0.at[2], q0.at[2], b, across))
    dzcopies, gcopies = [], []
    for d, to in zip(ds_of, peers):
        theirs = pl.ds(pl.multiple_of(rows * to, rows), rows)
        dzcopies.append(send(dzb.at[theirs, :], dzc.at[:, lanes], dzs.at[d], dzr.at[d], b, to))
    for d, to in zip(ds_of, peers):
        theirs = pl.ds(pl.multiple_of(rows * to, rows), rows)
        gcopies.append(send(gb.at[theirs, :], gc.at[:, lanes], gsd.at[d], grd.at[d], b, to))
    dzc[:, lanes] = dzb[mine, :]
    gc[:, lanes] = gb[mine, :]
    ocopy.wait()
    t[1152:] = (owno[...] + rxo[...].astype(F32)).astype(BF16)
    wcopies[1].wait()
    own[...] = gs[c].astype(F32) + ra[0].astype(F32)
    wcopies[2].wait()
    t[:1152] = (own[...] + rx[...].astype(F32)).astype(BF16)
    size = r1.shape[1]
    copies = []
    for d in range(1, groups):
        to = (q + d) % groups
        cut = pl.ds(pl.multiple_of(to * size, size), size)
        copies.append(send(t.at[cut], r1.at[q], s1.at[d], q1.at[d], to * ZLEN + z, c))
    r1[q] = t[pl.ds(pl.multiple_of(q * size, size), size)]
    for copy in copies:
        copy.wait()
    total = r1[0].astype(F32)
    for i in range(1, groups):
        total = total + r1[i].astype(F32)
    fs[...] = total.reshape(fs.shape)
    copies = []
    for d in range(1, ZLEN):
        to = (z + d) % ZLEN
        copies.append(send(fs.at[to], r2.at[z], s2.at[d], q2.at[d], q * ZLEN + to, c))
    r2[z] = fs[z]
    for copy in dzcopies:
        copy.wait()
    halo = [
        send(dzc.at[:, points - share : points], dext.at[:, :share], h2s.at[0], h2r.at[0], down, c),
        send(dzc.at[:, :share], dext.at[:, share + points :], h2s.at[1], h2r.at[1], up, c),
    ]
    for copy in copies:
        copy.wait()
    total = r2[0]
    for i in range(1, ZLEN):
        total = total + r2[i]
    fr[...] = total
    copies = []
    for d in range(1, ZLEN):
        to = (z + d) % ZLEN
        copies.append(send(fr, ag.at[z], s3.at[d], q3.at[d], q * ZLEN + to, c))
    ag[z] = total
    width = 384
    sums = [jnp.zeros((rows, 128), F32) for _ in range(3)]
    for at in range(0, points, width):
        grad = dzc[:, at : at + width].astype(F32)
        views = (
            shifted(ext, at + low // 128 * 128, low % 128, width),
            ext[:, at + share : at + share + width].astype(F32),
            shifted(ext, at + high // 128 * 128, high % 128, width),
        )
        for i in range(3):
            prod = views[i] * grad
            for o in range(0, width, 128):
                sums[i] = sums[i] + prod[:, o : o + 128]
    gkt[...] = jnp.zeros(gkt.shape, F32)
    for i in range(3):
        whole = jnp.sum(sums[i], axis=1, keepdims=True)
        gkt[i : i + 1, :rows] = jnp.sum(jnp.where(eye, whole, 0.0), axis=0, keepdims=True)

    def spread(i, _):
        send(gkt, gkr.at[b], ks, kr, (b + i) % bands, c)
        return 0

    lax.fori_loop(1, bands, spread, 0)
    gkr[b] = gkt[...]
    dext[:, share : share + points] = dzc[:, :points]
    for copy in copies:
        copy.wait()
    tb[...] = ag[...].reshape(size, 128).astype(BF16)
    copies = []
    for d in range(1, groups):
        to = (q + d) % groups
        cut = pl.ds(pl.multiple_of(q * size, size), size)
        copies.append(send(tb, out.at[cut], s4.at[d], q4.at[d], to * ZLEN + z, c))
    out[pl.ds(pl.multiple_of(q * size, size), size)] = tb[...]
    for copy in halo:
        copy.wait()

    @pl.when(b == 0)
    def _():
        dext[:, :share] = jnp.zeros((rows, share), BF16)

    @pl.when(b == bands - 1)
    def _():
        dext[:, share + points :] = jnp.zeros((rows, share), BF16)

    for copy in gcopies:
        copy.wait()
    for at in range(0, points, width):
        dat[:, at : at + width] = (
            gc[:, at : at + width].astype(F32)
            + t0 * shifted(dext, at + high // 128 * 128, high % 128, width)
            + t1 * dext[:, at + share : at + share + width].astype(F32)
            + t2 * shifted(dext, at + low // 128 * 128, low % 128, width)
        ).astype(BF16)
    drain(gkr.at[pl.ds(0, bands - 1)], kr)
    total = gkr[0]
    for i in range(1, bands):
        total = total + gkr[i]
    gkout[...] = total
    for copy in copies:
        copy.wait()
    drain(gkr.at[pl.ds(0, bands - 1)], ks)
    drain(sp.at[pl.ds(0, 2 * bands - 2)], ss)
    drain(bk.at[pl.ds(0, 2 * bands - 2)], rs)
    dstore.wait()


def local(
    atmos, kernels, w_one, w_two, w_flux, sea_mask, route,
    ocean_state, ct_atmos, ct_ocean, wo_one, wo_two,
):
    chans = lax.axis_size("chan")
    bands = lax.axis_size("band")
    rows, points = atmos.shape
    blocks = points // PTS
    own_blocks = -(-blocks // chans)
    share = own_blocks * PTS
    padded = own_blocks * chans
    quarter = PTS // chans
    slots = ocean_state.shape[2]
    hid = w_one.shape[2]
    full = rows * chans
    wide = wo_one.shape[1]
    total = wide * chans
    groups = bands // ZLEN
    flat = 1536
    big, little = 1152, 384
    size = flat // groups
    small = size // ZLEN
    vm = pl.BlockSpec(memory_space=VMEM)
    sm = pl.BlockSpec(memory_space=pltpu.SMEM)
    anywhere = pl.BlockSpec(memory_space=pl.ANY)

    table = pl.pallas_call(
        table_kernel,
        out_shape=jax.ShapeDtypeStruct((8, 128), jnp.int32),
        in_specs=[vm],
        out_specs=vm,
    )(route)
    ocean = VMEM((slots, quarter, PTS), BF16)
    points_first = VMEM((quarter, slots, PTS), BF16)
    wide_rows = VMEM((rows, padded * PTS), BF16)
    extended = VMEM((rows, points + 2 * share), BF16)
    square = VMEM((full, share), BF16)
    dat, dst, out, gk = pl.pallas_call(
        main_kernel,
        out_shape=[
            jax.ShapeDtypeStruct((rows, points), BF16),
            jax.ShapeDtypeStruct((quarter, slots, PTS), BF16),
            jax.ShapeDtypeStruct((flat, 128), BF16),
            jax.ShapeDtypeStruct((8, 128), F32),
        ],
        in_specs=[sm] + [vm] * 8 + [anywhere] * 3,
        out_specs=[vm, anywhere, vm, vm],
        scratch_shapes=[
            extended, wide_rows, wide_rows, square, square, square,
            VMEM((chans, full, hid), BF16),
            VMEM((chans, hid, full), BF16),
            VMEM((full, PTS), BF16),
            VMEM((own_blocks, PTS, PTS), BF16),
            VMEM((padded + 1, quarter, PTS), BF16),
            VMEM((1, padded * PTS), F32),
            VMEM((chans, hid, share), BF16),
            VMEM((chans, hid, share), BF16),
            wide_rows, square, ocean, ocean, ocean, ocean, points_first, points_first, points_first,
            VMEM((2 * PTS, total), BF16),
            VMEM((total, PTS), BF16),
            VMEM((2 * ZLEN * quarter, 2 * ZLEN * quarter), BF16),
            VMEM((2 * PTS, total), F32),
            VMEM((PTS, total), F32),
            VMEM((padded, quarter, PTS), BF16),
            VMEM((own_blocks, PTS, PTS), BF16),
            square, wide_rows, square, wide_rows, extended,
            VMEM((full, share), F32),
            VMEM((hid, share), BF16),
            VMEM((full, PTS), F32),
            VMEM((chans, big, 128), BF16),
            VMEM((2, big, 128), BF16),
            VMEM((big, 128), BF16),
            VMEM((big, 128), BF16),
            VMEM((chans, little, 128), BF16),
            VMEM((2, little, 128), BF16),
            VMEM((little, 128), BF16),
            VMEM((little, 128), BF16),
            VMEM((big, 128), F32),
            VMEM((little, 128), F32),
            VMEM((flat, 128), BF16),
            VMEM((groups, size, 128), BF16),
            VMEM((ZLEN, small, 128), F32),
            VMEM((ZLEN, small, 128), F32),
            VMEM((small, 128), F32),
            VMEM((ZLEN, small, 128), F32),
            VMEM((size, 128), BF16),
            VMEM((8, 128), F32),
            VMEM((bands, 8, 128), F32),
            DMA((4,)), DMA((2,)), DMA((2,)), DMA((3, 5)), DMA((3, 5)), DMA((4,)), DMA((4,)),
            DMA((3, 4)), DMA((3, 4)), DMA((3, 4)), DMA((3, 4)), DMA((4,)), DMA((4,)),
            DMA, DMA((groups,)), DMA, DMA,
            DMA((3,)), DMA((3,)), DMA((4,)), DMA((4,)), DMA((4,)), DMA((4,)), DMA((4,)), DMA((4,)),
            DMA((2,)), DMA((2,)), DMA((3,)), DMA((3,)),
            DMA((groups,)), DMA((groups,)), DMA((ZLEN,)), DMA((ZLEN,)),
            DMA((ZLEN,)), DMA((ZLEN,)), DMA((groups,)), DMA((groups,)), DMA, DMA,
        ],
        compiler_params=pltpu.CompilerParams(
            collective_id=0, has_side_effects=True, vmem_limit_bytes=LIMIT
        ),
    )(
        table, atmos, kernels[0], w_one[0], w_two[0], w_flux, sea_mask.reshape(1, points),
        wo_one, wo_two, ct_atmos, ocean_state, ct_ocean,
    )
    datmos, dk, dw1, dw2, dwf, dstate, do1, do2 = pl.pallas_call(
        finish_kernel,
        out_shape=[
            jax.ShapeDtypeStruct(dat.shape, BF16),
            jax.ShapeDtypeStruct((3, rows), F32),
            jax.ShapeDtypeStruct((full, hid), F32),
            jax.ShapeDtypeStruct((hid, full), F32),
            jax.ShapeDtypeStruct((rows, PTS), F32),
            jax.ShapeDtypeStruct(dst.shape, BF16),
            jax.ShapeDtypeStruct((2 * PTS, wide), F32),
            jax.ShapeDtypeStruct((wide, PTS), F32),
        ],
        in_specs=[vm] * 4,
        out_specs=[vm] * 8,
        compiler_params=pltpu.CompilerParams(vmem_limit_bytes=LIMIT // 2),
    )(dat, dst, out, gk)
    return datmos, dk[None], dw1[None], dw2[None], dwf, dstate[:, None], do1, do2


def solution(mesh):
    in_specs = (
        P("chan", "band"),
        P(None, None, "chan"),
        P(None, None, "chan"),
        P(None, "chan", None),
        P("chan", None),
        P("band"),
        P("band", None),
        P(None, "band", None, None),
        P("chan", "band"),
        P(None, "band", None, None),
        P(None, "chan"),
        P("chan", None),
    )
    out_specs = (
        P("chan", "band"),
        P(None, None, "chan"),
        P(None, None, "chan"),
        P(None, "chan", None),
        P("chan", None),
        P("chan", "band", None, None),
        P(None, "chan"),
        P("chan", None),
    )
    return jax.shard_map(local, mesh=mesh, in_specs=in_specs, out_specs=out_specs, check_vma=False)
```

time: 1260 us -> 169 us (0.13)
  waiting for transfers between devices: 713 us -> 0 us
  blocking collectives: 360 us -> 0 us
  Pallas kernels: 0 us -> 158 us
  matrix products: 63.9 us -> 0 us
  local copies, waits for them, and re-layouts: 50.4 us -> 8.54 us
  starting transfers between devices: 37.9 us -> 0 us
  between operations: 14.6 us -> 0.66 us
  other arithmetic: 13.4 us -> 0 us
    psum x1 -> x0, blocking collectives: 360 us -> none  [local(): lax.psum((jnp.stack(tap_grads), jnp.stack(one_grads), jnp.stack(two_grads...]
    psum x2 -> x0, waiting for transfers between devices: 347 us -> none  [the longest x1 293 us: local(): lax.psum((jnp.stack(tap_grads), jnp.stack(one_grads), jnp.stack(two_grads...]
    pallas_call x0 -> x3, Pallas kernels: none -> 158 us  [the longest x1 155 us: local(): pl.pallas_call(main_kernel, out_shape=[jax.ShapeDtypeStruct((rows, points...]
    reduce_scatter x4 -> x0, waiting for transfers between devices: 138 us -> none  [chan_share(): lax.psum_scatter(for_sending(terms), 'chan', scatter_dimension=0, tiled=T...]
    all_to_all x2 -> x0, waiting for transfers between devices: 122 us -> none  [couple(): lax.all_to_all(blocks, 'band', split_axis=1, concat_axis=1, tiled=True)]
    all_gather x3 -> x0, waiting for transfers between devices: 96.2 us -> none  [whole_chan(): return lax.all_gather(field, 'chan', axis=0, tiled=True)]
    dot_general x19 -> x0, matrix products: 63.9 us -> none  [the longest x14 55.7 us: contract(): lax.dot_general(left, right, (((left_dim,), (right_dim,)), ((), ())), pre...]
    all_to_all x2 -> x0, starting transfers between devices: 26.1 us -> none  [couple(): lax.all_to_all(blocks, 'band', split_axis=1, concat_axis=1, tiled=True)]
  transfers between devices with their start and end apart: 15 -> 0, of which waited for: 15 -> 0; matrix products, arithmetic and copies ran while one was open for 4% -> 0% of each run, Pallas kernels for 0% -> 0%
where the time goes in v2:
time: 169 us; the launch traced here: 167 us
  Pallas kernels  158 us (93%)
  local copies, waits for them, and re-layouts  8.54 us (5%)
    pallas_call x1, Pallas kernels, local(): pl.pallas_call(main_kernel, out_shape=[jax.ShapeDtypeStruct((rows, points...  155 us
    unnamed x11, local copies, waits for them, and re-layouts  7.18 us

profile of v2, /device:TPU:8, one launch (start us, length us, event | category | flops | bytes accessed | tf_op | source)
XLA Modules:
  0.0 167.4 jit_solution(18342081253735365698)
XLA Ops:
  0.6 1.3 copy.25
  1.9 1.4 reshape.19.sea
  3.3 1.4 copy.20.route
  4.6 1.6 shard_map.179.table
  6.2 155.2 %shard_map.180 = (bf16[64,5760]{1,0:T(8,128)(2,1)}, bf16[32,128,128]{2,1,0:T(8,128)(2,1)}, bf16[1536,128]{1,0:T(8,128)(2,1)}, f32[8,128]{1,0:T(8,128)}) custom-call(s32[8,128]{1,0:T(8,128)} %shard_map.179.table, bf16[64,5760]{1,0:T(8,128)(2,1)} %atmos.1, f32[3,64]{1,0:T(4,128)} %bitcast.14, bf16[256,256]{1,0:T(8,128)(2,1)} %bitcast.12, ...), custom_call_target="tpu_custom_call" | custom-call | tf_op jit(solution)/shard_map/pallas_call | solution.py:556
  161.4 0.0 copy-start
  161.4 1.2 copy-done
  162.6 0.0 copy-start.1
  162.6 1.1 copy-done.1
  163.7 0.0 copy-start.2
  163.7 1.0 copy-done.2
  164.7 0.0 copy-start.3
  164.7 0.7 copy-done.3
  165.4 1.5 shard_map.181
  166.9 0.6 copy.21
Async XLA Ops:
  161.4 1.2 copy-start
  162.6 1.1 copy-start.1
  163.7 1.0 copy-start.2
  164.7 0.7 copy-start.3

commit v3 on v2

v3 whole, which is shorter than its diff:
```python
import functools

import jax
import jax.numpy as jnp
from jax import lax
from jax.experimental import pallas as pl
from jax.experimental.pallas import tpu as pltpu
from jax.sharding import PartitionSpec as P

PTS = 128
LON = 1440
MESH = pl.DeviceIdType.MESH
F32 = jnp.float32
BF16 = jnp.bfloat16
VMEM = pltpu.VMEM
DMA = pltpu.SemaphoreType.DMA
ZLEN = 8
LIMIT = 56 * 1024 * 1024


def nn(a, b):
    return lax.dot_general(a, b, (((1,), (0,)), ((), ())), preferred_element_type=F32)


def tn(a, b):
    return lax.dot_general(a, b, (((0,), (0,)), ((), ())), preferred_element_type=F32)


def nt(a, b):
    return lax.dot_general(a, b, (((1,), (1,)), ((), ())), preferred_element_type=F32)


def sigmoid(v):
    return 0.5 * jnp.tanh(0.5 * v) + 0.5


def place():
    b, c = lax.axis_index("band"), lax.axis_index("chan")
    mate = (c // 2) * 2 + (1 - c % 2)
    return b, c, mate, (c + 2) % 4, (mate + 2) % 4


def send(src, dst, ssem, rsem, b, c):
    copy = pltpu.make_async_remote_copy(
        src_ref=src,
        dst_ref=dst,
        send_sem=ssem,
        recv_sem=rsem,
        device_id=(b, c),
        device_id_type=MESH,
    )
    copy.start()
    return copy


def drain(ref, sem):
    pltpu.make_async_copy(ref, ref, sem).wait()


def signal(b, c):
    pl.semaphore_signal(
        pltpu.get_barrier_semaphore(), inc=1, device_id=(b, c), device_id_type=MESH
    )


def taken(ref, start, width):
    extra = start % 128
    if extra == 0:
        return ref[:, start : start + width].astype(F32)
    wide = ref[:, start - extra : start - extra + width + 128].astype(F32)
    return pltpu.roll(wide, width + 128 - extra, axis=1)[:, :width]


def table_kernel(route, table):
    blocks = route.shape[1]
    row = route[...]
    k = lax.broadcasted_iota(jnp.int32, (blocks, blocks), 0)
    j = lax.broadcasted_iota(jnp.int32, (blocks, blocks), 1)
    col = jnp.sum(jnp.where(k == j, row, 0), axis=1, keepdims=True)
    rank = jnp.sum(jnp.where((row == col) & (j < k), 1, 0), axis=1, keepdims=True)
    slot = col * 2 + rank
    k = lax.broadcasted_iota(jnp.int32, (blocks, 128), 0)
    s = lax.broadcasted_iota(jnp.int32, (blocks, 128), 1)
    empty = blocks
    inv = empty + jnp.sum(jnp.where(slot == s, k - empty, 0), axis=0, keepdims=True)
    back = jnp.sum(jnp.where(k == s, slot, 0), axis=0, keepdims=True)
    line = lax.broadcasted_iota(jnp.int32, (8, 128), 0)
    table[...] = jnp.where(line == 0, inv, back)


def finish_kernel(dat, dst, out, datmos, dk, dw1, dw2, dwf, dstate, do1, do2):
    datmos[...] = dat[...]
    dstate[...] = dst[...]
    for j in range(2):
        dw1[:, j * 128 : j * 128 + 128] = out[j * 256 : j * 256 + 256].astype(F32)
        dw2[:, j * 128 : j * 128 + 128] = out[512 + j * 256 : 768 + j * 256].astype(F32)
    dwf[...] = out[1024:1088].astype(F32)
    do1[...] = out[1152:1408].astype(F32)
    do2[...] = out[1408:1536].astype(F32).T
    tile = out[1088:1152].astype(F32).T
    for i in range(3):
        dk[i] = tile[i : i + 1, :]


def main_kernel(
    table, atmos, taps, w_one, w_two, w_flux, sea, wo_one, wo_two, ct_all, state_all, cot_all,
    dat, dst, out,
    al, cl, ext, zb, alm, tapt, tapr, tapf, w1, w2, wf, fx, fm, mk, mk4, hid, slope,
    ctv0, ctb, sp, rf, bk, rb, st, ctv, ds, wa, wb, perm, go1, go2,
    dfp, dfb, gb, dext, dl, dq, dzacc, dubuf, gwf, gkp, gkr,
    gs, ra, hx, rx, gso, rao, hxo, rxo, own, owno, t, r1, fs, r2, fr, ag, tb,
    lsem, hs, hr, ws, wr, ts, tr, as_, ar, fxs, fxr, cs, cr, ss, sr, rs, rr,
    os_, or_, dfs, dfr, h2s, h2r, gks, gkq, das, dar, s0, q0, s1, q1, s2, q2, s3, q3, s4, q4,
):
    b, c, mate, across, diag = place()
    bands = lax.axis_size("band")
    up, down = (b + bands - 1) % bands, (b + 1) % bands
    q, z = b // ZLEN, b % ZLEN
    groups = bands // ZLEN
    flip = ((q // 2) * 2 + (1 - q % 2)) * ZLEN + z
    rows, points = atmos.shape
    full, share = zb.shape
    lats = points // LON
    width = share // lats
    quarter = st.shape[0]
    blocks = dfp.shape[0]
    row_groups = LON // quarter
    few = row_groups // 4
    stride = few * quarter
    wide = wo_one.shape[1]
    peers = [(c + 2) % 4, (c + 1) % 4, (c + 3) % 4]
    order = (2, 1, 3)
    pairs = list(zip(order, peers))

    def greet(i, _):
        signal((b + i) % bands, c)
        return 0

    for d in (1, 2, 3):
        signal(b, (c + d) % 4)
    signal(flip, across)
    lax.fori_loop(1, bands, greet, 0)
    loads = [
        pltpu.make_async_copy(ct_all, ctv0, lsem.at[0]),
        pltpu.make_async_copy(
            state_all.at[pl.ds(pl.multiple_of(quarter * c, quarter), quarter), 0], st, lsem.at[1]
        ),
        pltpu.make_async_copy(
            cot_all.at[pl.ds(pl.multiple_of(quarter * c, quarter), quarter), 0], ctv, lsem.at[2]
        ),
    ]
    for load in loads:
        load.start()
    mine = pl.ds(pl.multiple_of(c * rows, rows), rows)
    eye = lax.broadcasted_iota(jnp.int32, (rows, rows), 0) == lax.broadcasted_iota(
        jnp.int32, (rows, rows), 1
    )
    for r in (0, lats - 1) + tuple(range(1, lats - 1)):
        for j in range(4):
            al[j, :, r * width : (r + 1) * width] = taken(
                atmos, r * LON + j * stride, width
            ).astype(BF16)
    tapt[...] = jnp.zeros(tapt.shape, F32)
    for i in range(3):
        tapt[i : i + 1, :rows] = taps[i]
    pl.semaphore_wait(pltpu.get_barrier_semaphore(), bands - 1 + 4)

    cuts = (
        slice(0, width), slice((lats - 1) * width, lats * width), slice(width, (lats - 1) * width)
    )
    acopies = [[], [], []]

    def send_state(k):
        lo, hi = cuts[k].start, cuts[k].stop
        for d, to in pairs:
            acopies[k].append(
                send(
                    al.at[to, :, lo:hi], ext.at[mine, width + lo : width + hi],
                    as_.at[k, d], ar.at[k, d], b, to,
                )
            )

    send_state(0)
    send_state(1)
    mine_wide = pl.ds(pl.multiple_of(c * wide, wide), wide)
    theirs = pl.ds(pl.multiple_of(across * rows, rows), rows)
    theirs_wide = pl.ds(pl.multiple_of(across * wide, wide), wide)
    sources = (w_one, w_two, w_flux, wo_one, wo_two)
    near = (w1.at[c], w2.at[c], wf.at[mine, :], wa.at[:, mine_wide], wb.at[mine_wide, :])
    far = (
        w1.at[across], w2.at[across], wf.at[theirs, :],
        wa.at[:, theirs_wide], wb.at[theirs_wide, :],
    )
    first, second, third, tcopies = [], [], [], []
    for i in range(5):
        second.append(send(sources[i], near[i], ws.at[1, i], wr.at[1, i], flip, across))
        first.append(send(sources[i], near[i], ws.at[0, i], wr.at[0, i], b, mate))
    for d, to in pairs:
        tcopies.append(send(tapt, tapr.at[c], ts.at[d], tr.at[d], b, to))
    send_state(2)
    w1[c] = w_one[...]
    w2[c] = w_two[...]
    wf[mine, :] = w_flux[...]
    wa[:, mine_wide] = wo_one[...]
    wb[mine_wide, :] = wo_two[...]
    ext[mine, width : width + share] = al[c]
    tapr[c] = tapt[...]
    for i in range(points // PTS):
        mk[:, i * PTS : (i + 1) * PTS] = sea[i : i + 1, :].astype(F32)
    for r in range(lats):
        for j in range(4):
            mk4[j, :, r * width : (r + 1) * width] = taken(mk, r * LON + j * stride, width)
    for k in (0, 1):
        for copy in acopies[k]:
            copy.wait()
    halo = [
        send(
            ext.at[:, lats * width : (lats + 1) * width], ext.at[:, :width],
            hs.at[0], hr.at[0], down, c,
        ),
        send(
            ext.at[:, width : 2 * width], ext.at[:, (lats + 1) * width :],
            hs.at[1], hr.at[1], up, c,
        ),
    ]
    for copy in tcopies:
        copy.wait()
    for j in range(4):
        for i in range(3):
            tapf[j * rows : (j + 1) * rows, i : i + 1] = jnp.sum(
                jnp.where(eye, tapr[j, i : i + 1, :rows], 0.0), axis=1, keepdims=True
            )
    t0, t1, t2 = tapf[:, 0:1], tapf[:, 1:2], tapf[:, 2:3]
    lane = lax.broadcasted_iota(jnp.int32, (1, share), 1) % width
    kept = jnp.where((lane < stride) | (c == 3), 1.0, 0.0)
    sea_kept = mk4[c] * kept
    for i in range(5):
        second[i].wait_recv()
        third.append(send(far[i], far[i], ws.at[2, i], wr.at[2, i], b, mate))
    for copy in acopies[2]:
        copy.wait()
    for i in range(3):
        first[i].wait()
        second[i].wait_send()
        third[i].wait()
    fcopies = []
    line = (1, 2, 0, 3)
    for r in line:
        if r == 0:
            for copy in halo:
                copy.wait()

            @pl.when(b == 0)
            def _():
                ext[:, :width] = jnp.zeros((full, width), BF16)

            @pl.when(b == bands - 1)
            def _():
                ext[:, (lats + 1) * width :] = jnp.zeros((full, width), BF16)

        cols = slice(r * width, (r + 1) * width)
        state = ext[:, (r + 1) * width : (r + 2) * width].astype(F32)
        zcol = (
            t0 * ext[:, r * width : (r + 1) * width].astype(F32)
            + t1 * state
            + t2 * ext[:, (r + 2) * width : (r + 3) * width].astype(F32)
        ).astype(BF16)
        zb[:, cols] = zcol
        total = None
        for i in range(4):
            u = tn(w1[i], zcol)
            sig = sigmoid(u)
            act = u * sig
            h = act.astype(BF16)
            hid[i, :, cols] = h
            slope[i, :, cols] = (sig + act * (1.0 - sig)).astype(BF16)
            piece = tn(w2[i], h)
            total = piece if total is None else total + piece
        acol = (state + total).astype(BF16)
        acol = (acol.astype(F32) * sea_kept[:, cols]).astype(BF16)
        alm[:, cols] = acol
        fx[r] = tn(acol, wf[...]).astype(BF16).reshape(fx.shape[1:])
        for d, to in pairs:
            i0 = (to + 3 * r + c) % 4
            k0 = (row_groups * r + few * c + i0) // 4
            twice = ((i0 + 1) // 4) * ((6 - c) // 4)
            k2 = k0 + 2 + twice * (blocks + 1 + 4 * c + r - k0 - 2)
            fcopies.append(
                send(
                    fx.at[r, 0:2, i0], fm.at[pl.ds(k0, 2)], fxs.at[r, d, 0], fxr.at[r, d, 0], b, to
                )
            )
            fcopies.append(
                send(
                    fx.at[r, 2:3, i0], fm.at[pl.ds(k2, 1)], fxs.at[r, d, 1], fxr.at[r, d, 1], b, to
                )
            )
        i0 = (2 * c + 3 * r) % 4
        k0 = (row_groups * r + few * c + i0) // 4
        twice = ((i0 + 1) // 4) * ((6 - c) // 4)
        k2 = k0 + 2 + twice * (blocks + 1 + 4 * c + r - k0 - 2)
        fm[pl.ds(k0, 2)] = fx[r, 0:2, i0]
        fm[k2] = fx[r, 2, i0]
    fm[blocks] = jnp.zeros(fm.shape[1:], BF16)
    span = 2 * ZLEN
    size = span * quarter
    r = lax.broadcasted_iota(jnp.int32, (size, size), 0)
    k = lax.broadcasted_iota(jnp.int32, (size, size), 1)
    perm[...] = jnp.where((r % span) * quarter + r // span == k, 1.0, 0.0).astype(BF16)
    go1[...] = jnp.zeros(go1.shape, F32)
    go2[...] = jnp.zeros(go2.shape, F32)
    for load in loads:
        load.wait()
    for i in range(3, 5):
        first[i].wait()
        second[i].wait_send()
        third[i].wait()
    for copy in fcopies:
        copy.wait()

    def pack(s, _):
        sp[s] = fm[table[0, s]]
        return 0

    lax.fori_loop(0, 2 * bands, pack, 0)
    turn = [(z + i) % ZLEN for i in range(ZLEN)]

    def couple(d, start):
        base = ((q + d) % groups) * ZLEN
        for i in range(start, ZLEN):
            to = base + turn[i]
            send(sp.at[pl.ds(2 * to, 2)], rf.at[pl.ds(2 * b, 2)], ss, sr.at[d], to, c)

    couple(0, 1)

    def couple_all(d, _):
        couple(d, 0)
        return 0

    lax.fori_loop(1, groups, couple_all, 0)
    rf[pl.ds(2 * b, 2)] = sp[pl.ds(2 * b, 2)]
    for r in range(lats):
        for j in range(4):
            cl[j, :, r * width : (r + 1) * width] = taken(
                ctv0, r * LON + j * stride, width
            ).astype(BF16)
    ctcopies = []
    for d, to in pairs:
        ctcopies.append(send(cl.at[to], ctb.at[mine, :], cs.at[d], cr.at[d], b, to))
    ctb[mine, :] = cl[c]
    drain(rf.at[pl.ds(0, span - 2)], sr.at[0])

    def step(d, _):
        @pl.when(d > 0)
        def _():
            drain(rf.at[pl.ds(0, span)], sr.at[d])

        src = (q + groups - d) % groups
        at = pl.ds(pl.multiple_of(src * span, span), span)
        force = nn(perm[...], rf[at].reshape(size, PTS)).astype(BF16)
        both = jnp.concatenate([st[:, at, :].reshape(size, PTS), force], axis=1)
        cot = ctv[:, at, :].reshape(size, PTS)
        pre = nn(both, wa[...])
        sig = sigmoid(pre)
        act = pre * sig
        grad = (nt(cot, wb[...]) * (sig + act * (1.0 - sig))).astype(BF16)
        back = nt(grad, wa[...])
        bk[at] = tn(perm[...], back[:, PTS:].astype(BF16)).astype(BF16).reshape(span, quarter, PTS)

        def give(i):
            to = src * ZLEN + turn[i]
            send(bk.at[pl.ds(2 * to, 2)], rb.at[pl.ds(2 * b, 2)], rs, rr, to, c)

        @pl.when(d > 0)
        def _():
            give(0)

        for i in range(1, ZLEN):
            give(i)
        ds[:, at, :] = (
            (cot.astype(F32) + back[:, :PTS]).astype(BF16).reshape(quarter, span, PTS)
        )
        go2[...] += tn(cot, act.astype(BF16))
        go1[...] += tn(both, grad)
        return 0

    lax.fori_loop(0, groups, step, 0)
    dstore = pltpu.make_async_copy(ds, dst, lsem.at[3])
    dstore.start()
    rb[pl.ds(2 * b, 2)] = bk[pl.ds(2 * b, 2)]
    for i in range(4):
        gso[i, :256] = go1[:, i * 128 : i * 128 + 128].astype(BF16)
        gso[i, 256:] = go2[:, i * 128 : i * 128 + 128].astype(BF16)
    ocopies = [
        send(gso.at[diag], rao.at[1], os_.at[1], or_.at[1], b, mate),
        send(gso.at[mate], rao.at[0], os_.at[0], or_.at[0], b, mate),
    ]
    for copy in ctcopies:
        copy.wait()
    drain(rb.at[pl.ds(0, 2 * bands - 2)], rr)

    def unpack(k, _):
        dfp[k] = rb[table[1, k]]
        return 0

    lax.fori_loop(0, blocks, unpack, 0)
    dcopies = []
    for r in range(lats):
        for d, to in pairs:
            i0 = (c + 3 * r + to) % 4
            k0 = (row_groups * r + few * to + i0) // 4
            dcopies.append(
                send(dfp.at[pl.ds(k0, 3)], dfb.at[r, :, i0], dfs.at[r, d], dfr.at[r, d], b, to)
            )
        i0 = (2 * c + 3 * r) % 4
        k0 = (row_groups * r + few * c + i0) // 4
        dfb[r, :, i0] = dfp[pl.ds(k0, 3)]
    for copy in ocopies:
        copy.wait()
    hxo[...] = (gso[across].astype(F32) + rao[1].astype(F32)).astype(BF16)
    owno[...] = gso[c].astype(F32) + rao[0].astype(F32)
    ocopy = send(hxo, rxo, os_.at[2], or_.at[2], b, across)
    gs[:, 1088:] = jnp.zeros((4, 64, 128), BF16)
    for copy in dcopies:
        copy.wait()
    flux = dfb[...].reshape(share, PTS)
    gb[...] = (ctb[...].astype(F32) * kept + nt(wf[...], flux) * sea_kept).astype(BF16)
    gwf[...] = nn(alm[...], flux)
    wcopies = []
    halo = []
    for turn, i in enumerate((diag, mate, across, c)):
        for r in (0, 3, 1, 2):
            cols = slice(r * width, (r + 1) * width)
            du = (nn(w2[i], gb[:, cols]) * slope[i, :, cols].astype(F32)).astype(BF16)
            dubuf[:, cols] = du
            piece = nn(w1[i], du)
            if turn == 0:
                dzacc[:, cols] = piece
            elif turn < 3:
                dzacc[:, cols] += piece
            else:
                at = (r + 1) * width
                dext[:, at : at + width] = (dzacc[:, cols] + piece).astype(BF16)
                if r == 0:
                    halo.append(
                        send(
                            dext.at[:, at : at + width], dext.at[:, (lats + 1) * width :],
                            h2s.at[1], h2r.at[1], up, c,
                        )
                    )
                if r == 3:
                    halo.append(
                        send(
                            dext.at[:, at : at + width], dext.at[:, :width],
                            h2s.at[0], h2r.at[0], down, c,
                        )
                    )
        g1 = nt(zb[...], dubuf[...])
        g2 = nt(hid[i], gb[...])
        for j in range(2):
            gs[i, j * 256 : j * 256 + 256] = g1[:, j * 128 : j * 128 + 128].astype(BF16)
            gs[i, 512 + j * 256 : 768 + j * 256] = g2[:, j * 128 : j * 128 + 128].astype(BF16)
        gs[i, 1024:1088] = gwf[pl.ds(pl.multiple_of(rows * i, rows), rows), :].astype(BF16)
        if turn == 0:
            wcopies.append(send(gs.at[diag], ra.at[1], s0.at[1], q0.at[1], b, mate))
        if turn == 1:
            wcopies.append(send(gs.at[mate], ra.at[0], s0.at[0], q0.at[0], b, mate))
        if turn == 2:
            wcopies[0].wait()
            hx[...] = (gs[across].astype(F32) + ra[1].astype(F32)).astype(BF16)
            wcopies.append(send(hx, rx, s0.at[2], q0.at[2], b, across))
    column = lax.broadcasted_iota(jnp.int32, (full, 128), 1)
    tile = jnp.zeros((full, 128), F32)
    for i in range(3):
        acc = jnp.zeros((full, 128), F32)
        for r in range(lats):
            prod = ext[:, (r + i) * width : (r + i + 1) * width].astype(F32) * dext[
                :, (r + 1) * width : (r + 2) * width
            ].astype(F32)
            for o in range(0, width, 128):
                acc = acc + prod[:, o : o + 128]
        tile = jnp.where(column == i, jnp.sum(acc, axis=1, keepdims=True), tile)
    gkp[...] = tile.reshape(gkp.shape)
    kcopies = []
    for d, to in pairs:
        kcopies.append(send(gkp.at[to], gkr.at[d], gks.at[d], gkq.at[d], b, to))
    dcopies = []

    def spread(r):
        cols = slice(r * width, (r + 1) * width)
        dl[:, cols] = (
            gb[:, cols].astype(F32)
            + t0 * dext[:, (r + 2) * width : (r + 3) * width].astype(F32)
            + t1 * dext[:, (r + 1) * width : (r + 2) * width].astype(F32)
            + t2 * dext[:, r * width : (r + 1) * width].astype(F32)
        ).astype(BF16)

    def send_back(k):
        lo, hi = cuts[k].start, cuts[k].stop
        for d, to in pairs:
            theirs = pl.ds(pl.multiple_of(rows * to, rows), rows)
            dcopies.append(
                send(dl.at[theirs, lo:hi], dq.at[c, :, lo:hi], das.at[k, d], dar.at[k, d], b, to)
            )

    spread(1)
    spread(2)
    send_back(2)
    wcopies[1].wait()
    own[...] = gs[c].astype(F32) + ra[0].astype(F32)
    ocopy.wait()
    t[1152:] = (owno[...] + rxo[...].astype(F32)).astype(BF16)
    for copy in kcopies:
        copy.wait()
    t[1088:1152] = (gkp[c] + gkr[1] + gkr[2] + gkr[3]).astype(BF16)
    wcopies[2].wait()
    t[:1088] = (own[:1088] + rx[:1088].astype(F32)).astype(BF16)
    size = r1.shape[1]
    copies = []
    for d in range(1, groups):
        to = (q + d) % groups
        cut = pl.ds(pl.multiple_of(to * size, size), size)
        copies.append(send(t.at[cut], r1.at[q], s1.at[d], q1.at[d], to * ZLEN + z, c))
    r1[q] = t[pl.ds(pl.multiple_of(q * size, size), size)]
    for copy in halo:
        copy.wait()

    @pl.when(b == 0)
    def _():
        dext[:, :width] = jnp.zeros((full, width), BF16)

    @pl.when(b == bands - 1)
    def _():
        dext[:, (lats + 1) * width :] = jnp.zeros((full, width), BF16)

    spread(0)
    send_back(0)
    spread(3)
    send_back(1)
    dq[c] = dl[mine, :]
    for copy in copies:
        copy.wait()
    total = r1[0].astype(F32)
    for i in range(1, groups):
        total = total + r1[i].astype(F32)
    fs[...] = total.reshape(fs.shape)
    copies = []
    for d in range(1, ZLEN):
        to = (z + d) % ZLEN
        copies.append(send(fs.at[to], r2.at[z], s2.at[d], q2.at[d], q * ZLEN + to, c))
    r2[z] = fs[z]
    for copy in copies:
        copy.wait()
    total = r2[0]
    for i in range(1, ZLEN):
        total = total + r2[i]
    fr[...] = total
    copies = []
    for d in range(1, ZLEN):
        to = (z + d) % ZLEN
        copies.append(send(fr, ag.at[z], s3.at[d], q3.at[d], q * ZLEN + to, c))
    ag[z] = total
    for copy in copies:
        copy.wait()
    tb[...] = ag[...].reshape(size, 128).astype(BF16)
    copies = []
    for d in range(1, groups):
        to = (q + d) % groups
        cut = pl.ds(pl.multiple_of(q * size, size), size)
        copies.append(send(tb, out.at[cut], s4.at[d], q4.at[d], to * ZLEN + z, c))
    out[pl.ds(pl.multiple_of(q * size, size), size)] = tb[...]
    for copy in dcopies:
        copy.wait()
    for r in range(lats):
        for j in range(4):
            start = r * LON + j * stride
            extra = start % 128
            piece = dq[j, :, r * width : (r + 1) * width]
            if extra == 0:
                dat[:, start : start + width] = piece
                continue
            base = start - extra
            moved = jnp.concatenate([piece.astype(F32), jnp.zeros((rows, 128), F32)], axis=1)
            moved = pltpu.roll(moved, extra, axis=1)
            lead = lax.broadcasted_iota(jnp.int32, (rows, 128), 1)
            dat[:, base : base + 128] = jnp.where(
                lead < extra, dat[:, base : base + 128].astype(F32), moved[:, :128]
            ).astype(BF16)
            dat[:, base + 128 : base + 128 + width] = moved[:, 128:].astype(BF16)
    for copy in copies:
        copy.wait()
    drain(sp.at[pl.ds(0, 2 * bands - 2)], ss)
    drain(bk.at[pl.ds(0, 2 * bands - 2)], rs)
    dstore.wait()


def local(
    atmos, kernels, w_one, w_two, w_flux, sea_mask, route,
    ocean_state, ct_atmos, ct_ocean, wo_one, wo_two,
):
    chans = lax.axis_size("chan")
    bands = lax.axis_size("band")
    rows, points = atmos.shape
    blocks = points // PTS
    quarter = PTS // chans
    lats = points // LON
    share = lats * (LON // quarter // chans + 1) * quarter
    width = share // lats
    slots = ocean_state.shape[2]
    hid = w_one.shape[2]
    full = rows * chans
    wide = wo_one.shape[1]
    total = wide * chans
    groups = bands // ZLEN
    flat = 1536
    big, little = 1152, 384
    size = flat // groups
    small = size // ZLEN
    vm = pl.BlockSpec(memory_space=VMEM)
    sm = pl.BlockSpec(memory_space=pltpu.SMEM)
    anywhere = pl.BlockSpec(memory_space=pl.ANY)

    table = pl.pallas_call(
        table_kernel,
        out_shape=jax.ShapeDtypeStruct((8, 128), jnp.int32),
        in_specs=[vm],
        out_specs=vm,
    )(route.T)
    ocean = VMEM((slots, quarter, PTS), BF16)
    points_first = VMEM((quarter, slots, PTS), BF16)
    split = VMEM((chans, rows, share), BF16)
    extended = VMEM((full, share + 2 * width), BF16)
    square = VMEM((full, share), BF16)
    grouped = VMEM((lats, width // PTS, chans, quarter, PTS), BF16)
    dat, dst, out = pl.pallas_call(
        main_kernel,
        out_shape=[
            jax.ShapeDtypeStruct((rows, points), BF16),
            jax.ShapeDtypeStruct((quarter, slots, PTS), BF16),
            jax.ShapeDtypeStruct((flat, 128), BF16),
        ],
        in_specs=[sm] + [vm] * 8 + [anywhere] * 3,
        out_specs=[vm, anywhere, vm],
        scratch_shapes=[
            split, split, extended, square, square,
            VMEM((8, 128), F32),
            VMEM((chans, 8, 128), F32),
            VMEM((full, 128), F32),
            VMEM((chans, full, hid), BF16),
            VMEM((chans, hid, full), BF16),
            VMEM((full, PTS), BF16),
            grouped,
            VMEM((blocks + 1 + 4 * lats, quarter, PTS), BF16),
            VMEM((1, points), F32),
            VMEM((chans, 1, share), F32),
            VMEM((chans, hid, share), BF16),
            VMEM((chans, hid, share), BF16),
            VMEM((rows, points), BF16),
            square, ocean, ocean, ocean, ocean, points_first, points_first, points_first,
            VMEM((2 * PTS, total), BF16),
            VMEM((total, PTS), BF16),
            VMEM((2 * ZLEN * quarter, 2 * ZLEN * quarter), BF16),
            VMEM((2 * PTS, total), F32),
            VMEM((PTS, total), F32),
            VMEM((blocks, quarter, PTS), BF16),
            grouped, square, extended, square, split,
            VMEM((full, share), F32),
            VMEM((hid, share), BF16),
            VMEM((full, PTS), F32),
            VMEM((chans, rows, 128), F32),
            VMEM((chans, rows, 128), F32),
            VMEM((chans, big, 128), BF16),
            VMEM((2, big, 128), BF16),
            VMEM((big, 128), BF16),
            VMEM((big, 128), BF16),
            VMEM((chans, little, 128), BF16),
            VMEM((2, little, 128), BF16),
            VMEM((little, 128), BF16),
            VMEM((little, 128), BF16),
            VMEM((big, 128), F32),
            VMEM((little, 128), F32),
            VMEM((flat, 128), BF16),
            VMEM((groups, size, 128), BF16),
            VMEM((ZLEN, small, 128), F32),
            VMEM((ZLEN, small, 128), F32),
            VMEM((small, 128), F32),
            VMEM((ZLEN, small, 128), F32),
            VMEM((size, 128), BF16),
            DMA((4,)), DMA((2,)), DMA((2,)), DMA((3, 5)), DMA((3, 5)), DMA((4,)), DMA((4,)),
            DMA((3, 4)), DMA((3, 4)), DMA((lats, 4, 2)), DMA((lats, 4, 2)), DMA((4,)), DMA((4,)),
            DMA, DMA((groups,)), DMA, DMA,
            DMA((3,)), DMA((3,)), DMA((lats, 4)), DMA((lats, 4)), DMA((2,)), DMA((2,)),
            DMA((4,)), DMA((4,)), DMA((3, 4)), DMA((3, 4)), DMA((3,)), DMA((3,)),
            DMA((groups,)), DMA((groups,)), DMA((ZLEN,)), DMA((ZLEN,)),
            DMA((ZLEN,)), DMA((ZLEN,)), DMA((groups,)), DMA((groups,)),
        ],
        compiler_params=pltpu.CompilerParams(
            collective_id=0, has_side_effects=True, vmem_limit_bytes=LIMIT
        ),
    )(
        table, atmos, kernels.transpose(1, 0, 2), w_one[0], w_two[0], w_flux, sea_mask.reshape(blocks, PTS),
        wo_one, wo_two, ct_atmos, ocean_state, ct_ocean,
    )
    datmos, dk, dw1, dw2, dwf, dstate, do1, do2 = pl.pallas_call(
        finish_kernel,
        out_shape=[
            jax.ShapeDtypeStruct(dat.shape, BF16),
            jax.ShapeDtypeStruct((3, 1, rows), F32),
            jax.ShapeDtypeStruct((full, hid), F32),
            jax.ShapeDtypeStruct((hid, full), F32),
            jax.ShapeDtypeStruct((rows, PTS), F32),
            jax.ShapeDtypeStruct(dst.shape, BF16),
            jax.ShapeDtypeStruct((2 * PTS, wide), F32),
            jax.ShapeDtypeStruct((wide, PTS), F32),
        ],
        in_specs=[vm] * 3,
        out_specs=[vm] * 8,
        compiler_params=pltpu.CompilerParams(vmem_limit_bytes=LIMIT + (4 << 20)),
    )(dat, dst, out)
    return datmos, dk.transpose(1, 0, 2), dw1[None], dw2[None], dwf, dstate[:, None], do1, do2


def solution(mesh):
    in_specs = (
        P("chan", "band"),
        P(None, None, "chan"),
        P(None, None, "chan"),
        P(None, "chan", None),
        P("chan", None),
        P("band"),
        P("band", None),
        P(None, "band", None, None),
        P("chan", "band"),
        P(None, "band", None, None),
        P(None, "chan"),
        P("chan", None),
    )
    out_specs = (
        P("chan", "band"),
        P(None, None, "chan"),
        P(None, None, "chan"),
        P(None, "chan", None),
        P("chan", None),
        P("chan", "band", None, None),
        P(None, "chan"),
        P("chan", None),
    )
    return jax.shard_map(local, mesh=mesh, in_specs=in_specs, out_specs=out_specs, check_vma=False)
```

time: 169 us -> 145 us (0.86)
  Pallas kernels: 158 us -> 144 us
  local copies, waits for them, and re-layouts: 8.54 us -> 0 us
    pallas_call x1, Pallas kernels: 155 us -> 140 us  [local(): pl.pallas_call(main_kernel, out_shape=[jax.ShapeDtypeStruct((rows, points...]
    unnamed x11 -> x0, local copies, waits for them, and re-layouts: 7.18 us -> none
where the time goes in v3:
time: 145 us
  Pallas kernels  144 us (99%)
    pallas_call x1, Pallas kernels, local(): pl.pallas_call(main_kernel, out_shape=[jax.ShapeDtypeStruct((rows, points...  140 us
    pallas_call x1, Pallas kernels, local(): pl.pallas_call(finish_kernel, out_shape=[jax.ShapeDtypeStruct(dat.shape,...  3.03 us

profile of v3, /device:TPU:8, one launch (start us, length us, event | category | flops | bytes accessed | tf_op | source)
XLA Modules:
  0.0 144.7 jit_solution(11800576798128298685)
XLA Ops:
  0.6 1.4 shard_map.179.table
  2.1 139.6 %shard_map.180 = (bf16[64,5760]{1,0:T(8,128)(2,1)}, bf16[32,128,128]{2,1,0:T(8,128)(2,1)}, bf16[1536,128]{1,0:T(8,128)(2,1)}) custom-call(s32[8,128]{1,0:T(8,128)} %shard_map.179.table, bf16[64,5760]{1,0:T(8,128)(2,1)} %atmos.1, f32[3,1,64]{2,1,0:T(1,128)} %bitcast.14, bf16[256,256]{1,0:T(8,128)(2,1)} %bitcast.11, bf16[256,256]{1,0:T(8,128)(2,1)} %bitcast.12, ...), custom_call_target="tpu_custom_call" | custom-call | tf_op jit(solution)/shard_map/pallas_call | solution.py:635
  141.7 3.0 %shard_map.181 = (bf16[64,5760]{1,0:T(8,128)(2,1)}, f32[3,1,64]{2,1,0:T(1,128)}, f32[256,256]{1,0:T(8,128)}, f32[256,256]{1,0:T(8,128)}, f32[64,128]{1,0:T(8,128...) custom-call(bf16[64,5760]{1,0:T(8,128)(2,1)} %get-tuple-element.19.dat, ...), custom_call_target="tpu_custom_call" | custom-call | tf_op jit(solution)/shard_map/pallas_call | solution.py:704

commit v4 on v3

--- a/solution.py
+++ b/solution.py
@@ -88,28 +88,50 @@
     table[...] = jnp.where(line == 0, inv, back)
 
 
-def finish_kernel(dat, dst, out, datmos, dk, dw1, dw2, dwf, dstate, do1, do2):
-    datmos[...] = dat[...]
-    dstate[...] = dst[...]
-    for j in range(2):
-        dw1[:, j * 128 : j * 128 + 128] = out[j * 256 : j * 256 + 256].astype(F32)
-        dw2[:, j * 128 : j * 128 + 128] = out[512 + j * 256 : 768 + j * 256].astype(F32)
-    dwf[...] = out[1024:1088].astype(F32)
-    do1[...] = out[1152:1408].astype(F32)
-    do2[...] = out[1408:1536].astype(F32).T
-    tile = out[1088:1152].astype(F32).T
+def finish_kernel(
+    dat, dst, out_hbm, datmos, dk, dw1, dw2, dwf, dstate, do1, do2, dbuf, sbuf, out, isem, osem
+):
+    loads = [
+        pltpu.make_async_copy(out_hbm, out, isem.at[0]),
+        pltpu.make_async_copy(dst, sbuf, isem.at[1]),
+        pltpu.make_async_copy(dat, dbuf, isem.at[2]),
+    ]
+    for load in loads:
+        load.start()
+    stores = [
+        pltpu.make_async_copy(sbuf, dstate, osem.at[0]),
+        pltpu.make_async_copy(dbuf, datmos, osem.at[1]),
+    ]
+    loads[0].wait()
+    half = out.shape[0] // 2
+    dw1[:, :128] = out[:256].astype(F32)
+    dw1[:, 128:] = out[256:512].astype(F32)
+    dw2[:32, :128] = out[512:544].astype(F32)
+    dw2[32:, :128] = out[half : half + 224].astype(F32)
+    dw2[:, 128:] = out[half + 224 : half + 480].astype(F32)
+    loads[1].wait()
+    stores[0].start()
+    loads[2].wait()
+    stores[1].start()
+    dwf[...] = out[half + 480 : half + 544].astype(F32)
+    tile = out[544:560].astype(F32) + out[half + 544 : half + 560].astype(F32)
     for i in range(3):
-        dk[i] = tile[i : i + 1, :]
+        dk[i] = tile[i : i + 1, :64]
+    do1[:192] = out[576:768].astype(F32)
+    do1[192:] = out[half + 576 : half + 640].astype(F32)
+    do2[...] = out[half + 640 :].astype(F32).T
+    for store in stores:
+        store.wait()
 
 
 def main_kernel(
-    table, atmos, taps, w_one, w_two, w_flux, sea, wo_one, wo_two, ct_all, state_all, cot_all,
-    dat, dst, out,
-    al, cl, ext, zb, alm, tapt, tapr, tapf, w1, w2, wf, fx, fm, mk, mk4, hid, slope,
+    table, taps, sea, atmos_all, w_one, w_two, w_flux, wo_one, wo_two, ct_all, state_all, cot_all,
+    dat_all, dst, out,
+    atmos, dat, al, cl, ext, zb, alm, tapt, tapr, tapf, w1, w2, wf, fx, fm, mk, mk4, hid, slope,
     ctv0, ctb, sp, rf, bk, rb, st, ctv, ds, wa, wb, perm, go1, go2,
     dfp, dfb, gb, dext, dl, dq, dzacc, dubuf, gwf, gkp, gkr,
-    gs, ra, hx, rx, gso, rao, hxo, rxo, own, owno, t, r1, fs, r2, fr, ag, tb,
-    lsem, hs, hr, ws, wr, ts, tr, as_, ar, fxs, fxr, cs, cr, ss, sr, rs, rr,
+    gs, ra, hx, rw, gso, rao, hxo, rxo, own, owno, ownb, ownob, t, r1, fs, r2, fr, ag, tb,
+    lsem, msem, hs, hr, ws, wr, ts, tr, as_, ar, fxs, fxr, cs, cr, ss, sr, rs, rr,
     os_, or_, dfs, dfr, h2s, h2r, gks, gkq, das, dar, s0, q0, s1, q1, s2, q2, s3, q3, s4, q4,
 ):
     b, c, mate, across, diag = place()
@@ -149,9 +171,16 @@
             cot_all.at[pl.ds(pl.multiple_of(quarter * c, quarter), quarter), 0], ctv, lsem.at[2]
         ),
     ]
-    for load in loads:
+    mine = pl.ds(pl.multiple_of(c * rows, rows), rows)
+    mine_wide = pl.ds(pl.multiple_of(c * wide, wide), wide)
+    sources = (w_one, w_two, w_flux, wo_one, wo_two)
+    near = (w1.at[c], w2.at[c], wf.at[mine, :], wa.at[:, mine_wide], wb.at[mine_wide, :])
+    early = [pltpu.make_async_copy(atmos_all, atmos, msem.at[5])]
+    for i in range(5):
+        early.append(pltpu.make_async_copy(sources[i], near[i], msem.at[i]))
+    for load in early + loads:
         load.start()
-    mine = pl.ds(pl.multiple_of(c * rows, rows), rows)
+    early[0].wait()
     eye = lax.broadcasted_iota(jnp.int32, (rows, rows), 0) == lax.broadcasted_iota(
         jnp.int32, (rows, rows), 1
     )
@@ -182,27 +211,20 @@
 
     send_state(0)
     send_state(1)
-    mine_wide = pl.ds(pl.multiple_of(c * wide, wide), wide)
     theirs = pl.ds(pl.multiple_of(across * rows, rows), rows)
     theirs_wide = pl.ds(pl.multiple_of(across * wide, wide), wide)
-    sources = (w_one, w_two, w_flux, wo_one, wo_two)
-    near = (w1.at[c], w2.at[c], wf.at[mine, :], wa.at[:, mine_wide], wb.at[mine_wide, :])
     far = (
         w1.at[across], w2.at[across], wf.at[theirs, :],
         wa.at[:, theirs_wide], wb.at[theirs_wide, :],
     )
     first, second, third, tcopies = [], [], [], []
     for i in range(5):
-        second.append(send(sources[i], near[i], ws.at[1, i], wr.at[1, i], flip, across))
-        first.append(send(sources[i], near[i], ws.at[0, i], wr.at[0, i], b, mate))
+        early[i + 1].wait()
+        second.append(send(near[i], near[i], ws.at[1, i], wr.at[1, i], flip, across))
+        first.append(send(near[i], near[i], ws.at[0, i], wr.at[0, i], b, mate))
     for d, to in pairs:
         tcopies.append(send(tapt, tapr.at[c], ts.at[d], tr.at[d], b, to))
     send_state(2)
-    w1[c] = w_one[...]
-    w2[c] = w_two[...]
-    wf[mine, :] = w_flux[...]
-    wa[:, mine_wide] = wo_one[...]
-    wb[mine_wide, :] = wo_two[...]
     ext[mine, width : width + share] = al[c]
     tapr[c] = tapt[...]
     for i in range(points // PTS):
@@ -417,18 +439,28 @@
         dfb[r, :, i0] = dfp[pl.ds(k0, 3)]
     for copy in ocopies:
         copy.wait()
+    side = q % 2
+    little, big = rxo.shape[1], rw.shape[1]
+    kept_little = pl.ds(pl.multiple_of(little * side, little), little)
+    sent_little = pl.ds(pl.multiple_of(little * (1 - side), little), little)
+    kept_big = pl.ds(pl.multiple_of(big * side, big), big)
+    sent_big = pl.ds(pl.multiple_of(big * (1 - side), big), big)
     hxo[...] = (gso[across].astype(F32) + rao[1].astype(F32)).astype(BF16)
     owno[...] = gso[c].astype(F32) + rao[0].astype(F32)
-    ocopy = send(hxo, rxo, os_.at[2], or_.at[2], b, across)
-    gs[:, 1088:] = jnp.zeros((4, 64, 128), BF16)
+    ownob[...] = owno[sent_little].astype(BF16)
     for copy in dcopies:
         copy.wait()
+    ocopies = [
+        send(ownob, rxo.at[2], os_.at[4], or_.at[4], flip, c),
+        send(hxo.at[kept_little], rxo.at[0], os_.at[2], or_.at[2], b, across),
+        send(hxo.at[sent_little], rxo.at[1], os_.at[3], or_.at[3], flip, across),
+    ]
     flux = dfb[...].reshape(share, PTS)
     gb[...] = (ctb[...].astype(F32) * kept + nt(wf[...], flux) * sea_kept).astype(BF16)
     gwf[...] = nn(alm[...], flux)
     wcopies = []
     halo = []
-    for turn, i in enumerate((diag, mate, across, c)):
+    for turn, i in enumerate((mate, c, diag, across)):
         for r in (0, 3, 1, 2):
             cols = slice(r * width, (r + 1) * width)
             du = (nn(w2[i], gb[:, cols]) * slope[i, :, cols].astype(F32)).astype(BF16)
@@ -462,15 +494,20 @@
             gs[i, 512 + j * 256 : 768 + j * 256] = g2[:, j * 128 : j * 128 + 128].astype(BF16)
         gs[i, 1024:1088] = gwf[pl.ds(pl.multiple_of(rows * i, rows), rows), :].astype(BF16)
         if turn == 0:
-            wcopies.append(send(gs.at[diag], ra.at[1], s0.at[1], q0.at[1], b, mate))
+            mcopies = [send(gs.at[mate], ra.at[0], s0.at[0], q0.at[0], b, mate)]
         if turn == 1:
-            wcopies.append(send(gs.at[mate], ra.at[0], s0.at[0], q0.at[0], b, mate))
+            mcopies[0].wait()
+            own[...] = gs[c].astype(F32) + ra[0].astype(F32)
+            ownb[...] = own[sent_big].astype(BF16)
+            wcopies.append(send(ownb, rw.at[2], s0.at[4], q0.at[4], flip, c))
         if turn == 2:
-            wcopies[0].wait()
+            mcopies.append(send(gs.at[diag], ra.at[1], s0.at[1], q0.at[1], b, mate))
+        if turn == 3:
+            mcopies[1].wait()
             hx[...] = (gs[across].astype(F32) + ra[1].astype(F32)).astype(BF16)
-            wcopies.append(send(hx, rx, s0.at[2], q0.at[2], b, across))
-    column = lax.broadcasted_iota(jnp.int32, (full, 128), 1)
-    tile = jnp.zeros((full, 128), F32)
+            wcopies.append(send(hx.at[kept_big], rw.at[0], s0.at[2], q0.at[2], b, across))
+            wcopies.append(send(hx.at[sent_big], rw.at[1], s0.at[3], q0.at[3], flip, across))
+    gkp[...] = jnp.zeros(gkp.shape, F32)
     for i in range(3):
         acc = jnp.zeros((full, 128), F32)
         for r in range(lats):
@@ -479,8 +516,11 @@
             ].astype(F32)
             for o in range(0, width, 128):
                 acc = acc + prod[:, o : o + 128]
-        tile = jnp.where(column == i, jnp.sum(acc, axis=1, keepdims=True), tile)
-    gkp[...] = tile.reshape(gkp.shape)
+        acc = jnp.sum(acc, axis=1, keepdims=True)
+        for j in range(4):
+            gkp[j, i : i + 1, :rows] = jnp.sum(
+                jnp.where(eye, acc[j * rows : (j + 1) * rows], 0.0), axis=0, keepdims=True
+            )
     kcopies = []
     for d, to in pairs:
         kcopies.append(send(gkp.at[to], gkr.at[d], gks.at[d], gkq.at[d], b, to))
@@ -505,23 +545,33 @@
 
     spread(1)
     spread(2)
-    send_back(2)
-    wcopies[1].wait()
-    own[...] = gs[c].astype(F32) + ra[0].astype(F32)
-    ocopy.wait()
-    t[1152:] = (owno[...] + rxo[...].astype(F32)).astype(BF16)
+    for copy in ocopies:
+        copy.wait()
+    t[big + 32 :] = (
+        owno[kept_little]
+        + rxo[0].astype(F32)
+        + rxo[1].astype(F32)
+        + rxo[2].astype(F32)
+    ).astype(BF16)
     for copy in kcopies:
         copy.wait()
-    t[1088:1152] = (gkp[c] + gkr[1] + gkr[2] + gkr[3]).astype(BF16)
-    wcopies[2].wait()
-    t[:1088] = (own[:1088] + rx[:1088].astype(F32)).astype(BF16)
+    t[big : big + 16] = (gkp[c] + gkr[1] + gkr[2] + gkr[3]).astype(BF16)
+    t[big + 16 : big + 32] = jnp.zeros((16, 128), BF16)
+    for copy in wcopies:
+        copy.wait()
+    t[:big] = (
+        own[kept_big] + rw[0].astype(F32) + rw[1].astype(F32) + rw[2].astype(F32)
+    ).astype(BF16)
     size = r1.shape[1]
+    x, xs = q // 2, groups // 2
     copies = []
-    for d in range(1, groups):
-        to = (q + d) % groups
+    for d in range(1, xs):
+        to = (x + d) % xs
         cut = pl.ds(pl.multiple_of(to * size, size), size)
-        copies.append(send(t.at[cut], r1.at[q], s1.at[d], q1.at[d], to * ZLEN + z, c))
-    r1[q] = t[pl.ds(pl.multiple_of(q * size, size), size)]
+        copies.append(
+            send(t.at[cut], r1.at[x], s1.at[d], q1.at[d], (2 * to + side) * ZLEN + z, c)
+        )
+    r1[x] = t[pl.ds(pl.multiple_of(x * size, size), size)]
     for copy in halo:
         copy.wait()
 
@@ -534,20 +584,20 @@
         dext[:, (lats + 1) * width :] = jnp.zeros((full, width), BF16)
 
     spread(0)
-    send_back(0)
     spread(3)
-    send_back(1)
     dq[c] = dl[mine, :]
     for copy in copies:
         copy.wait()
     total = r1[0].astype(F32)
-    for i in range(1, groups):
+    for i in range(1, xs):
         total = total + r1[i].astype(F32)
     fs[...] = total.reshape(fs.shape)
     copies = []
     for d in range(1, ZLEN):
         to = (z + d) % ZLEN
         copies.append(send(fs.at[to], r2.at[z], s2.at[d], q2.at[d], q * ZLEN + to, c))
+    for k in range(3):
+        send_back(k)
     r2[z] = fs[z]
     for copy in copies:
         copy.wait()
@@ -564,11 +614,11 @@
         copy.wait()
     tb[...] = ag[...].reshape(size, 128).astype(BF16)
     copies = []
+    cut = pl.ds(pl.multiple_of((side * xs + x) * size, size), size)
     for d in range(1, groups):
         to = (q + d) % groups
-        cut = pl.ds(pl.multiple_of(q * size, size), size)
         copies.append(send(tb, out.at[cut], s4.at[d], q4.at[d], to * ZLEN + z, c))
-    out[pl.ds(pl.multiple_of(q * size, size), size)] = tb[...]
+    out[cut] = tb[...]
     for copy in dcopies:
         copy.wait()
     for r in range(lats):
@@ -587,11 +637,14 @@
                 lead < extra, dat[:, base : base + 128].astype(F32), moved[:, :128]
             ).astype(BF16)
             dat[:, base + 128 : base + 128 + width] = moved[:, 128:].astype(BF16)
+    astore = pltpu.make_async_copy(dat, dat_all, lsem.at[4])
+    astore.start()
     for copy in copies:
         copy.wait()
     drain(sp.at[pl.ds(0, 2 * bands - 2)], ss)
     drain(bk.at[pl.ds(0, 2 * bands - 2)], rs)
     dstore.wait()
+    astore.wait()
 
 
 def local(
@@ -613,7 +666,7 @@
     total = wide * chans
     groups = bands // ZLEN
     flat = 1536
-    big, little = 1152, 384
+    big, little = 1088, 384
     size = flat // groups
     small = size // ZLEN
     vm = pl.BlockSpec(memory_space=VMEM)
@@ -639,9 +692,11 @@
             jax.ShapeDtypeStruct((quarter, slots, PTS), BF16),
             jax.ShapeDtypeStruct((flat, 128), BF16),
         ],
-        in_specs=[sm] + [vm] * 8 + [anywhere] * 3,
-        out_specs=[vm, anywhere, vm],
+        in_specs=[sm, vm, vm] + [anywhere] * 9,
+        out_specs=[anywhere, anywhere, vm],
         scratch_shapes=[
+            VMEM((rows, points), BF16),
+            VMEM((rows, points), BF16),
             split, split, extended, square, square,
             VMEM((8, 128), F32),
             VMEM((chans, 8, 128), F32),
@@ -667,30 +722,32 @@
             VMEM((full, share), F32),
             VMEM((hid, share), BF16),
             VMEM((full, PTS), F32),
-            VMEM((chans, rows, 128), F32),
-            VMEM((chans, rows, 128), F32),
+            VMEM((chans, 16, 128), F32),
+            VMEM((chans, 16, 128), F32),
             VMEM((chans, big, 128), BF16),
             VMEM((2, big, 128), BF16),
             VMEM((big, 128), BF16),
-            VMEM((big, 128), BF16),
+            VMEM((3, big // 2, 128), BF16),
             VMEM((chans, little, 128), BF16),
             VMEM((2, little, 128), BF16),
             VMEM((little, 128), BF16),
-            VMEM((little, 128), BF16),
+            VMEM((3, little // 2, 128), BF16),
             VMEM((big, 128), F32),
             VMEM((little, 128), F32),
-            VMEM((flat, 128), BF16),
-            VMEM((groups, size, 128), BF16),
+            VMEM((big // 2, 128), BF16),
+            VMEM((little // 2, 128), BF16),
+            VMEM((flat // 2, 128), BF16),
+            VMEM((groups // 2, size, 128), BF16),
             VMEM((ZLEN, small, 128), F32),
             VMEM((ZLEN, small, 128), F32),
             VMEM((small, 128), F32),
             VMEM((ZLEN, small, 128), F32),
             VMEM((size, 128), BF16),
-            DMA((4,)), DMA((2,)), DMA((2,)), DMA((3, 5)), DMA((3, 5)), DMA((4,)), DMA((4,)),
+            DMA((5,)), DMA((6,)), DMA((2,)), DMA((2,)), DMA((3, 5)), DMA((3, 5)), DMA((4,)), DMA((4,)),
             DMA((3, 4)), DMA((3, 4)), DMA((lats, 4, 2)), DMA((lats, 4, 2)), DMA((4,)), DMA((4,)),
             DMA, DMA((groups,)), DMA, DMA,
-            DMA((3,)), DMA((3,)), DMA((lats, 4)), DMA((lats, 4)), DMA((2,)), DMA((2,)),
-            DMA((4,)), DMA((4,)), DMA((3, 4)), DMA((3, 4)), DMA((3,)), DMA((3,)),
+            DMA((5,)), DMA((5,)), DMA((lats, 4)), DMA((lats, 4)), DMA((2,)), DMA((2,)),
+            DMA((4,)), DMA((4,)), DMA((3, 4)), DMA((3, 4)), DMA((5,)), DMA((5,)),
             DMA((groups,)), DMA((groups,)), DMA((ZLEN,)), DMA((ZLEN,)),
             DMA((ZLEN,)), DMA((ZLEN,)), DMA((groups,)), DMA((groups,)),
         ],
@@ -698,8 +755,8 @@
             collective_id=0, has_side_effects=True, vmem_limit_bytes=LIMIT
         ),
     )(
-        table, atmos, kernels.transpose(1, 0, 2), w_one[0], w_two[0], w_flux, sea_mask.reshape(blocks, PTS),
-        wo_one, wo_two, ct_atmos, ocean_state, ct_ocean,
+        table, kernels.transpose(1, 0, 2), sea_mask.reshape(blocks, PTS), atmos, w_one[0], w_two[0],
+        w_flux, wo_one, wo_two, ct_atmos, ocean_state, ct_ocean,
     )
     datmos, dk, dw1, dw2, dwf, dstate, do1, do2 = pl.pallas_call(
         finish_kernel,
@@ -713,8 +770,11 @@
             jax.ShapeDtypeStruct((2 * PTS, wide), F32),
             jax.ShapeDtypeStruct((wide, PTS), F32),
         ],
-        in_specs=[vm] * 3,
-        out_specs=[vm] * 8,
+        in_specs=[anywhere] * 3,
+        out_specs=[anywhere, vm, vm, vm, vm, anywhere, vm, vm],
+        scratch_shapes=[
+            VMEM(dat.shape, BF16), VMEM(dst.shape, BF16), VMEM(out.shape, BF16), DMA((3,)), DMA((2,)),
+        ],
         compiler_params=pltpu.CompilerParams(vmem_limit_bytes=LIMIT + (4 << 20)),
     )(dat, dst, out)
     return datmos, dk.transpose(1, 0, 2), dw1[None], dw2[None], dwf, dstate[:, None], do1, do2

time: 145 us -> 137 us (0.945)
  Pallas kernels: 144 us -> 136 us
    pallas_call x1, Pallas kernels: 140 us -> 131 us  [local(): pl.pallas_call(main_kernel, out_shape=[jax.ShapeDtypeStruct((rows, points...]
where the time goes in v4:
time: 137 us
  Pallas kernels  136 us (99%)
    pallas_call x1, Pallas kernels, local(): pl.pallas_call(main_kernel, out_shape=[jax.ShapeDtypeStruct((rows, points...  131 us
    pallas_call x1, Pallas kernels, local(): pl.pallas_call(finish_kernel, out_shape=[jax.ShapeDtypeStruct(dat.shape,...  3.46 us

profile of v4, /device:TPU:8, one launch (start us, length us, event | category | flops | bytes accessed | tf_op | source)
XLA Modules:
  0.0 136.8 jit_solution(14492370917129392563)
XLA Ops:
  0.6 1.4 %shard_map.179.table = s32[8,128]{1,0:T(8,128)} custom-call(s32[1,45]{1,0:T(1,128)} %bitcast.15), custom_call_target="tpu_custom_call" | custom-call | tf_op jit(solution)/shard_map/pallas_call | solution.py:676
  2.1 131.1 %shard_map.180 = (bf16[64,5760]{1,0:T(8,128)(2,1)}, bf16[32,128,128]{2,1,0:T(8,128)(2,1)}, bf16[1536,128]{1,0:T(8,128)(2,1)}) custom-call(s32[8,128]{1,0:T(8,128)} %shard_map.179.table, f32[3,1,64]{2,1,0:T(1,128)} %bitcast.14, s32[45,128]{1,0:T(8,128)} %bitcast.13, bf16[64,5760]{1,0:T(8,128)(2,1)} %atmos_all.1, bf16[256,256]{1,0:T(8,128)(2,1)} %bitcast.11, ...), custom_call_target="tpu_custom_call" | custom-call | tf_op jit(solution)/shard_map/pallas_call | solution.py:688
  133.2 3.5 %shard_map.181 = (bf16[64,5760]{1,0:T(8,128)(2,1)}, f32[3,1,64]{2,1,0:T(1,128)}, f32[256,256]{1,0:T(8,128)}, f32[256,256]{1,0:T(8,128)}, f32[64,128]{1,0:T(8,128...) custom-call(bf16[64,5760]{1,0:T(8,128)(2,1)} %get-tuple-element.19.dat, ...), custom_call_target="tpu_custom_call" | custom-call | tf_op jit(solution)/shard_map/pallas_call | solution.py:761

commit v5 on v4

--- a/solution.py
+++ b/solution.py
@@ -71,9 +71,8 @@
     return pltpu.roll(wide, width + 128 - extra, axis=1)[:, :width]
 
 
-def table_kernel(route, table):
-    blocks = route.shape[1]
-    row = route[...]
+def tables(row):
+    blocks = row.shape[1]
     k = lax.broadcasted_iota(jnp.int32, (blocks, blocks), 0)
     j = lax.broadcasted_iota(jnp.int32, (blocks, blocks), 1)
     col = jnp.sum(jnp.where(k == j, row, 0), axis=1, keepdims=True)
@@ -81,38 +80,21 @@
     slot = col * 2 + rank
     k = lax.broadcasted_iota(jnp.int32, (blocks, 128), 0)
     s = lax.broadcasted_iota(jnp.int32, (blocks, 128), 1)
-    empty = blocks
-    inv = empty + jnp.sum(jnp.where(slot == s, k - empty, 0), axis=0, keepdims=True)
+    inv = blocks + jnp.sum(jnp.where(slot == s, k - blocks, 0), axis=0, keepdims=True)
     back = jnp.sum(jnp.where(k == s, slot, 0), axis=0, keepdims=True)
     line = lax.broadcasted_iota(jnp.int32, (8, 128), 0)
-    table[...] = jnp.where(line == 0, inv, back)
-
-
-def finish_kernel(
-    dat, dst, out_hbm, datmos, dk, dw1, dw2, dwf, dstate, do1, do2, dbuf, sbuf, out, isem, osem
-):
-    loads = [
-        pltpu.make_async_copy(out_hbm, out, isem.at[0]),
-        pltpu.make_async_copy(dst, sbuf, isem.at[1]),
-        pltpu.make_async_copy(dat, dbuf, isem.at[2]),
-    ]
-    for load in loads:
-        load.start()
-    stores = [
-        pltpu.make_async_copy(sbuf, dstate, osem.at[0]),
-        pltpu.make_async_copy(dbuf, datmos, osem.at[1]),
-    ]
-    loads[0].wait()
+    return jnp.where(line == 0, inv, back)
+
+
+def finish_kernel(dat, dst, out, datmos, dk, dw1, dw2, dwf, dstate, do1, do2):
     half = out.shape[0] // 2
+    datmos[...] = dat[...]
+    dstate[...] = dst[...]
     dw1[:, :128] = out[:256].astype(F32)
     dw1[:, 128:] = out[256:512].astype(F32)
     dw2[:32, :128] = out[512:544].astype(F32)
     dw2[32:, :128] = out[half : half + 224].astype(F32)
     dw2[:, 128:] = out[half + 224 : half + 480].astype(F32)
-    loads[1].wait()
-    stores[0].start()
-    loads[2].wait()
-    stores[1].start()
     dwf[...] = out[half + 480 : half + 544].astype(F32)
     tile = out[544:560].astype(F32) + out[half + 544 : half + 560].astype(F32)
     for i in range(3):
@@ -120,14 +102,12 @@
     do1[:192] = out[576:768].astype(F32)
     do1[192:] = out[half + 576 : half + 640].astype(F32)
     do2[...] = out[half + 640 :].astype(F32).T
-    for store in stores:
-        store.wait()
 
 
 def main_kernel(
-    table, taps, sea, atmos_all, w_one, w_two, w_flux, wo_one, wo_two, ct_all, state_all, cot_all,
+    route, taps, sea, atmos_all, w_one, w_two, w_flux, wo_one, wo_two, ct_all, state_all, cot_all,
     dat_all, dst, out,
-    atmos, dat, al, cl, ext, zb, alm, tapt, tapr, tapf, w1, w2, wf, fx, fm, mk, mk4, hid, slope,
+    tabv, table, atmos, dat, al, cl, ext, zb, alm, tapt, tapr, tapf, w1, w2, wf, fx, fm, mk, mk4, hid, slope,
     ctv0, ctb, sp, rf, bk, rb, st, ctv, ds, wa, wb, perm, go1, go2,
     dfp, dfb, gb, dext, dl, dq, dzacc, dubuf, gwf, gkp, gkr,
     gs, ra, hx, rw, gso, rao, hxo, rxo, own, owno, ownb, ownob, t, r1, fs, r2, fr, ag, tb,
@@ -154,14 +134,20 @@
     order = (2, 1, 3)
     pairs = list(zip(order, peers))
 
-    def greet(i, _):
-        signal((b + i) % bands, c)
-        return 0
-
+    turn = [(z + i) % ZLEN for i in range(ZLEN)]
     for d in (1, 2, 3):
         signal(b, (c + d) % 4)
     signal(flip, across)
-    lax.fori_loop(1, bands, greet, 0)
+    for i in range(1, ZLEN):
+        signal(q * ZLEN + turn[i], c)
+
+    def greet(d, _):
+        base = ((q + d) % groups) * ZLEN
+        for i in range(ZLEN):
+            signal(base + turn[i], c)
+        return 0
+
+    lax.fori_loop(1, groups, greet, 0)
     loads = [
         pltpu.make_async_copy(ct_all, ctv0, lsem.at[0]),
         pltpu.make_async_copy(
@@ -180,6 +166,9 @@
         early.append(pltpu.make_async_copy(sources[i], near[i], msem.at[i]))
     for load in early + loads:
         load.start()
+    tabv[...] = tables(route[...])
+    tcopy = pltpu.make_async_copy(tabv, table, msem.at[6])
+    tcopy.start()
     early[0].wait()
     eye = lax.broadcasted_iota(jnp.int32, (rows, rows), 0) == lax.broadcasted_iota(
         jnp.int32, (rows, rows), 1
@@ -192,6 +181,7 @@
     tapt[...] = jnp.zeros(tapt.shape, F32)
     for i in range(3):
         tapt[i : i + 1, :rows] = taps[i]
+    tcopy.wait()
     pl.semaphore_wait(pltpu.get_barrier_semaphore(), bands - 1 + 4)
 
     cuts = (
@@ -224,27 +214,30 @@
         first.append(send(near[i], near[i], ws.at[0, i], wr.at[0, i], b, mate))
     for d, to in pairs:
         tcopies.append(send(tapt, tapr.at[c], ts.at[d], tr.at[d], b, to))
-    send_state(2)
     ext[mine, width : width + share] = al[c]
     tapr[c] = tapt[...]
+    for copy in acopies[0]:
+        copy.wait()
+    halo = [
+        send(
+            ext.at[:, width : 2 * width], ext.at[:, (lats + 1) * width :],
+            hs.at[1], hr.at[1], up, c,
+        )
+    ]
+    for copy in acopies[1]:
+        copy.wait()
+    halo.append(
+        send(
+            ext.at[:, lats * width : (lats + 1) * width], ext.at[:, :width],
+            hs.at[0], hr.at[0], down, c,
+        )
+    )
+    send_state(2)
     for i in range(points // PTS):
         mk[:, i * PTS : (i + 1) * PTS] = sea[i : i + 1, :].astype(F32)
     for r in range(lats):
         for j in range(4):
             mk4[j, :, r * width : (r + 1) * width] = taken(mk, r * LON + j * stride, width)
-    for k in (0, 1):
-        for copy in acopies[k]:
-            copy.wait()
-    halo = [
-        send(
-            ext.at[:, lats * width : (lats + 1) * width], ext.at[:, :width],
-            hs.at[0], hr.at[0], down, c,
-        ),
-        send(
-            ext.at[:, width : 2 * width], ext.at[:, (lats + 1) * width :],
-            hs.at[1], hr.at[1], up, c,
-        ),
-    ]
     for copy in tcopies:
         copy.wait()
     for j in range(4):
@@ -345,7 +338,6 @@
         return 0
 
     lax.fori_loop(0, 2 * bands, pack, 0)
-    turn = [(z + i) % ZLEN for i in range(ZLEN)]
 
     def couple(d, start):
         base = ((q + d) % groups) * ZLEN
@@ -427,7 +419,7 @@
 
     lax.fori_loop(0, blocks, unpack, 0)
     dcopies = []
-    for r in range(lats):
+    for r in (0, 3, 1, 2):
         for d, to in pairs:
             i0 = (c + 3 * r + to) % 4
             k0 = (row_groups * r + few * to + i0) // 4
@@ -448,16 +440,20 @@
     hxo[...] = (gso[across].astype(F32) + rao[1].astype(F32)).astype(BF16)
     owno[...] = gso[c].astype(F32) + rao[0].astype(F32)
     ownob[...] = owno[sent_little].astype(BF16)
-    for copy in dcopies:
-        copy.wait()
+    for n, r in enumerate((0, 3, 1, 2)):
+        for copy in dcopies[3 * n : 3 * n + 3]:
+            copy.wait()
+        cols = slice(r * width, (r + 1) * width)
+        flux = dfb[r].reshape(width, PTS)
+        gb[:, cols] = (
+            ctb[:, cols].astype(F32) * kept[:, cols] + nt(wf[...], flux) * sea_kept[:, cols]
+        ).astype(BF16)
     ocopies = [
         send(ownob, rxo.at[2], os_.at[4], or_.at[4], flip, c),
         send(hxo.at[kept_little], rxo.at[0], os_.at[2], or_.at[2], b, across),
         send(hxo.at[sent_little], rxo.at[1], os_.at[3], or_.at[3], flip, across),
     ]
-    flux = dfb[...].reshape(share, PTS)
-    gb[...] = (ctb[...].astype(F32) * kept + nt(wf[...], flux) * sea_kept).astype(BF16)
-    gwf[...] = nn(alm[...], flux)
+    gwf[...] = nn(alm[...], dfb[...].reshape(share, PTS))
     wcopies = []
     halo = []
     for turn, i in enumerate((mate, c, diag, across)):
@@ -571,6 +567,7 @@
         copies.append(
             send(t.at[cut], r1.at[x], s1.at[d], q1.at[d], (2 * to + side) * ZLEN + z, c)
         )
+    send_back(2)
     r1[x] = t[pl.ds(pl.multiple_of(x * size, size), size)]
     for copy in halo:
         copy.wait()
@@ -584,7 +581,9 @@
         dext[:, (lats + 1) * width :] = jnp.zeros((full, width), BF16)
 
     spread(0)
+    send_back(0)
     spread(3)
+    send_back(1)
     dq[c] = dl[mine, :]
     for copy in copies:
         copy.wait()
@@ -596,8 +595,6 @@
     for d in range(1, ZLEN):
         to = (z + d) % ZLEN
         copies.append(send(fs.at[to], r2.at[z], s2.at[d], q2.at[d], q * ZLEN + to, c))
-    for k in range(3):
-        send_back(k)
     r2[z] = fs[z]
     for copy in copies:
         copy.wait()
@@ -670,15 +667,8 @@
     size = flat // groups
     small = size // ZLEN
     vm = pl.BlockSpec(memory_space=VMEM)
-    sm = pl.BlockSpec(memory_space=pltpu.SMEM)
     anywhere = pl.BlockSpec(memory_space=pl.ANY)
 
-    table = pl.pallas_call(
-        table_kernel,
-        out_shape=jax.ShapeDtypeStruct((8, 128), jnp.int32),
-        in_specs=[vm],
-        out_specs=vm,
-    )(route.T)
     ocean = VMEM((slots, quarter, PTS), BF16)
     points_first = VMEM((quarter, slots, PTS), BF16)
     split = VMEM((chans, rows, share), BF16)
@@ -692,9 +682,11 @@
             jax.ShapeDtypeStruct((quarter, slots, PTS), BF16),
             jax.ShapeDtypeStruct((flat, 128), BF16),
         ],
-        in_specs=[sm, vm, vm] + [anywhere] * 9,
+        in_specs=[vm, vm, vm] + [anywhere] * 9,
         out_specs=[anywhere, anywhere, vm],
         scratch_shapes=[
+            VMEM((8, 128), jnp.int32),
+            pltpu.SMEM((8, 128), jnp.int32),
             VMEM((rows, points), BF16),
             VMEM((rows, points), BF16),
             split, split, extended, square, square,
@@ -743,7 +735,7 @@
             VMEM((small, 128), F32),
             VMEM((ZLEN, small, 128), F32),
             VMEM((size, 128), BF16),
-            DMA((5,)), DMA((6,)), DMA((2,)), DMA((2,)), DMA((3, 5)), DMA((3, 5)), DMA((4,)), DMA((4,)),
+            DMA((5,)), DMA((7,)), DMA((2,)), DMA((2,)), DMA((3, 5)), DMA((3, 5)), DMA((4,)), DMA((4,)),
             DMA((3, 4)), DMA((3, 4)), DMA((lats, 4, 2)), DMA((lats, 4, 2)), DMA((4,)), DMA((4,)),
             DMA, DMA((groups,)), DMA, DMA,
             DMA((5,)), DMA((5,)), DMA((lats, 4)), DMA((lats, 4)), DMA((2,)), DMA((2,)),
@@ -755,7 +747,7 @@
             collective_id=0, has_side_effects=True, vmem_limit_bytes=LIMIT
         ),
     )(
-        table, kernels.transpose(1, 0, 2), sea_mask.reshape(blocks, PTS), atmos, w_one[0], w_two[0],
+        route.T, kernels.transpose(1, 0, 2), sea_mask.reshape(blocks, PTS), atmos, w_one[0], w_two[0],
         w_flux, wo_one, wo_two, ct_atmos, ocean_state, ct_ocean,
     )
     datmos, dk, dw1, dw2, dwf, dstate, do1, do2 = pl.pallas_call(
@@ -770,11 +762,8 @@
             jax.ShapeDtypeStruct((2 * PTS, wide), F32),
             jax.ShapeDtypeStruct((wide, PTS), F32),
         ],
-        in_specs=[anywhere] * 3,
-        out_specs=[anywhere, vm, vm, vm, vm, anywhere, vm, vm],
-        scratch_shapes=[
-            VMEM(dat.shape, BF16), VMEM(dst.shape, BF16), VMEM(out.shape, BF16), DMA((3,)), DMA((2,)),
-        ],
+        in_specs=[vm] * 3,
+        out_specs=[vm] * 8,
         compiler_params=pltpu.CompilerParams(vmem_limit_bytes=LIMIT + (4 << 20)),
     )(dat, dst, out)
     return datmos, dk.transpose(1, 0, 2), dw1[None], dw2[None], dwf, dstate[:, None], do1, do2

time: 137 us -> 137 us (level)
    pallas_call x1, Pallas kernels: 131 us -> 133 us  [local(): pl.pallas_call(main_kernel, out_shape=[jax.ShapeDtypeStruct((rows, points...]
    pallas_call x1 -> x0, Pallas kernels: 1.44 us -> none  [local(): pl.pallas_call(table_kernel, out_shape=jax.ShapeDtypeStruct((8, 128), jnp...]
where the time goes in v5:
time: 137 us; the launch traced here: 136 us
  Pallas kernels  136 us (99%)
    pallas_call x1, Pallas kernels, local(): pl.pallas_call(main_kernel, out_shape=[jax.ShapeDtypeStruct((rows, points...  133 us
    pallas_call x1, Pallas kernels, local(): pl.pallas_call(finish_kernel, out_shape=[jax.ShapeDtypeStruct(dat.shape,...  3.02 us

profile of v5, /device:TPU:8, one launch (start us, length us, event | category | flops | bytes accessed | tf_op | source)
XLA Modules:
  0.0 136.4 jit_solution(13925999031193037305)
XLA Ops:
  0.6 132.7 %shard_map.179 = (bf16[64,5760]{1,0:T(8,128)(2,1)}, bf16[32,128,128]{2,1,0:T(8,128)(2,1)}, bf16[1536,128]{1,0:T(8,128)(2,1)}) custom-call(s32[1,45]{1,0:T(1,128)} %bitcast.15, f32[3,1,64]{2,1,0:T(1,128)} %bitcast.14, s32[45,128]{1,0:T(8,128)} %bitcast.13, bf16[64,5760]{1,0:T(8,128)(2,1)} %atmos_all.1, bf16[256,256]{1,0:T(8,128)(2,1)} %bitcast.11, ...), custom_call_target="tpu_custom_call" | custom-call | tf_op jit(solution)/shard_map/pallas_call | solution.py:678
  133.4 3.0 %shard_map.180 = (bf16[64,5760]{1,0:T(8,128)(2,1)}, f32[3,1,64]{2,1,0:T(1,128)}, f32[256,256]{1,0:T(8,128)}, f32[256,256]{1,0:T(8,128)}, f32[64,128]{1,0:T(8,128...) custom-call(bf16[64,5760]{1,0:T(8,128)(2,1)} %get-tuple-element.19.dat, ...), custom_call_target="tpu_custom_call" | custom-call | tf_op jit(solution)/shard_map/pallas_call | solution.py:753

commit v6 on v5

--- a/solution.py
+++ b/solution.py
@@ -134,20 +134,28 @@
     order = (2, 1, 3)
     pairs = list(zip(order, peers))
 
-    turn = [(z + i) % ZLEN for i in range(ZLEN)]
-    for d in (1, 2, 3):
+    z_far = (4, 3, 5, 2, 6, 1, 7)
+    turn = [(z + i) % ZLEN for i in z_far + (0,)]
+    x, xs, side = q // 2, groups // 2, q % 2
+
+    def column(n, way):
+        m = n % 4
+        dx = (2 + m + m // 2 + 2 * (m // 3)) % 4
+        dy = 1 - n // 4
+        return ((x + way * dx + xs) % xs) * 2 + (side + dy) % 2
+
+    def greet(n, _):
+        base = column(n, 1) * ZLEN
+        for to in turn:
+            signal(base + to, c)
+        return 0
+
+    lax.fori_loop(0, groups - 1, greet, 0)
+    for to in turn[:-1]:
+        signal(q * ZLEN + to, c)
+    signal(flip, across)
+    for d in (2, 1, 3):
         signal(b, (c + d) % 4)
-    signal(flip, across)
-    for i in range(1, ZLEN):
-        signal(q * ZLEN + turn[i], c)
-
-    def greet(d, _):
-        base = ((q + d) % groups) * ZLEN
-        for i in range(ZLEN):
-            signal(base + turn[i], c)
-        return 0
-
-    lax.fori_loop(1, groups, greet, 0)
     loads = [
         pltpu.make_async_copy(ct_all, ctv0, lsem.at[0]),
         pltpu.make_async_copy(
@@ -214,25 +222,31 @@
         first.append(send(near[i], near[i], ws.at[0, i], wr.at[0, i], b, mate))
     for d, to in pairs:
         tcopies.append(send(tapt, tapr.at[c], ts.at[d], tr.at[d], b, to))
+    send_state(2)
     ext[mine, width : width + share] = al[c]
     tapr[c] = tapt[...]
-    for copy in acopies[0]:
-        copy.wait()
-    halo = [
-        send(
-            ext.at[:, width : 2 * width], ext.at[:, (lats + 1) * width :],
-            hs.at[1], hr.at[1], up, c,
+    halo = []
+
+    def send_halo(k, d):
+        at = pl.ds(pl.multiple_of(rows * ((c + 4 - d) % 4), rows), rows)
+        if k == 0:
+            src, dst, to = (1, 2), (lats + 1, lats + 2), up
+        else:
+            src, dst, to = (lats, lats + 1), (0, 1), down
+        halo.append(
+            send(
+                ext.at[at, src[0] * width : src[1] * width],
+                ext.at[at, dst[0] * width : dst[1] * width],
+                hs.at[k, d], hr.at[k, d], to, c,
+            )
         )
-    ]
-    for copy in acopies[1]:
-        copy.wait()
-    halo.append(
-        send(
-            ext.at[:, lats * width : (lats + 1) * width], ext.at[:, :width],
-            hs.at[0], hr.at[0], down, c,
-        )
-    )
-    send_state(2)
+
+    send_halo(0, 0)
+    send_halo(1, 0)
+    for k in (0, 1):
+        for n, d in ((1, 1), (2, 3), (0, 2)):
+            acopies[k][n].wait()
+            send_halo(k, d)
     for i in range(points // PTS):
         mk[:, i * PTS : (i + 1) * PTS] = sea[i : i + 1, :].astype(F32)
     for r in range(lats):
@@ -339,19 +353,18 @@
 
     lax.fori_loop(0, 2 * bands, pack, 0)
 
-    def couple(d, start):
-        base = ((q + d) % groups) * ZLEN
-        for i in range(start, ZLEN):
-            to = base + turn[i]
-            send(sp.at[pl.ds(2 * to, 2)], rf.at[pl.ds(2 * b, 2)], ss, sr.at[d], to, c)
-
-    couple(0, 1)
-
-    def couple_all(d, _):
-        couple(d, 0)
+    def couple(n, ways):
+        base = column(n, 1) * ZLEN
+        for way in ways:
+            to = base + way
+            send(sp.at[pl.ds(2 * to, 2)], rf.at[pl.ds(2 * b, 2)], ss, sr.at[n], to, c)
+
+    def couple_all(n, _):
+        couple(n, turn)
         return 0
 
-    lax.fori_loop(1, groups, couple_all, 0)
+    lax.fori_loop(0, groups - 1, couple_all, 0)
+    couple(groups - 1, turn[:-1])
     rf[pl.ds(2 * b, 2)] = sp[pl.ds(2 * b, 2)]
     for r in range(lats):
         for j in range(4):
@@ -362,14 +375,17 @@
     for d, to in pairs:
         ctcopies.append(send(cl.at[to], ctb.at[mine, :], cs.at[d], cr.at[d], b, to))
     ctb[mine, :] = cl[c]
-    drain(rf.at[pl.ds(0, span - 2)], sr.at[0])
-
-    def step(d, _):
-        @pl.when(d > 0)
+
+    def step(n, _):
+        @pl.when(n < groups - 1)
         def _():
-            drain(rf.at[pl.ds(0, span)], sr.at[d])
-
-        src = (q + groups - d) % groups
+            drain(rf.at[pl.ds(0, span)], sr.at[n])
+
+        @pl.when(n == groups - 1)
+        def _():
+            drain(rf.at[pl.ds(0, span - 2)], sr.at[n])
+
+        src = column(n, -1)
         at = pl.ds(pl.multiple_of(src * span, span), span)
         force = nn(perm[...], rf[at].reshape(size, PTS)).astype(BF16)
         both = jnp.concatenate([st[:, at, :].reshape(size, PTS), force], axis=1)
@@ -381,16 +397,17 @@
         back = nt(grad, wa[...])
         bk[at] = tn(perm[...], back[:, PTS:].astype(BF16)).astype(BF16).reshape(span, quarter, PTS)
 
-        def give(i):
-            to = src * ZLEN + turn[i]
+        def give(way):
+            to = src * ZLEN + way
             send(bk.at[pl.ds(2 * to, 2)], rb.at[pl.ds(2 * b, 2)], rs, rr, to, c)
 
-        @pl.when(d > 0)
+        for way in turn[:-1]:
+            give(way)
+
+        @pl.when(n < groups - 1)
         def _():
-            give(0)
-
-        for i in range(1, ZLEN):
-            give(i)
+            give(turn[-1])
+
         ds[:, at, :] = (
             (cot.astype(F32) + back[:, :PTS]).astype(BF16).reshape(quarter, span, PTS)
         )
@@ -431,7 +448,6 @@
         dfb[r, :, i0] = dfp[pl.ds(k0, 3)]
     for copy in ocopies:
         copy.wait()
-    side = q % 2
     little, big = rxo.shape[1], rw.shape[1]
     kept_little = pl.ds(pl.multiple_of(little * side, little), little)
     sent_little = pl.ds(pl.multiple_of(little * (1 - side), little), little)
@@ -559,9 +575,8 @@
         own[kept_big] + rw[0].astype(F32) + rw[1].astype(F32) + rw[2].astype(F32)
     ).astype(BF16)
     size = r1.shape[1]
-    x, xs = q // 2, groups // 2
     copies = []
-    for d in range(1, xs):
+    for d in (2, 1, 3):
         to = (x + d) % xs
         cut = pl.ds(pl.multiple_of(to * size, size), size)
         copies.append(
@@ -592,7 +607,7 @@
         total = total + r1[i].astype(F32)
     fs[...] = total.reshape(fs.shape)
     copies = []
-    for d in range(1, ZLEN):
+    for d in z_far:
         to = (z + d) % ZLEN
         copies.append(send(fs.at[to], r2.at[z], s2.at[d], q2.at[d], q * ZLEN + to, c))
     r2[z] = fs[z]
@@ -603,7 +618,7 @@
         total = total + r2[i]
     fr[...] = total
     copies = []
-    for d in range(1, ZLEN):
+    for d in z_far:
         to = (z + d) % ZLEN
         copies.append(send(fr, ag.at[z], s3.at[d], q3.at[d], q * ZLEN + to, c))
     ag[z] = total
@@ -612,9 +627,8 @@
     tb[...] = ag[...].reshape(size, 128).astype(BF16)
     copies = []
     cut = pl.ds(pl.multiple_of((side * xs + x) * size, size), size)
-    for d in range(1, groups):
-        to = (q + d) % groups
-        copies.append(send(tb, out.at[cut], s4.at[d], q4.at[d], to * ZLEN + z, c))
+    for n in range(groups - 1):
+        copies.append(send(tb, out.at[cut], s4.at[n], q4.at[n], column(n, 1) * ZLEN + z, c))
     out[cut] = tb[...]
     for copy in dcopies:
         copy.wait()
@@ -735,7 +749,7 @@
             VMEM((small, 128), F32),
             VMEM((ZLEN, small, 128), F32),
             VMEM((size, 128), BF16),
-            DMA((5,)), DMA((7,)), DMA((2,)), DMA((2,)), DMA((3, 5)), DMA((3, 5)), DMA((4,)), DMA((4,)),
+            DMA((5,)), DMA((7,)), DMA((2, 4)), DMA((2, 4)), DMA((3, 5)), DMA((3, 5)), DMA((4,)), DMA((4,)),
             DMA((3, 4)), DMA((3, 4)), DMA((lats, 4, 2)), DMA((lats, 4, 2)), DMA((4,)), DMA((4,)),
             DMA, DMA((groups,)), DMA, DMA,
             DMA((5,)), DMA((5,)), DMA((lats, 4)), DMA((lats, 4)), DMA((2,)), DMA((2,)),

time: 137 us -> 132 us (0.964)
  Pallas kernels: 136 us -> 131 us
    pallas_call x1, Pallas kernels: 133 us -> 128 us  [local(): pl.pallas_call(main_kernel, out_shape=[jax.ShapeDtypeStruct((rows, points...]
where the time goes in v6:
time: 132 us; the launch traced here: 131 us
  Pallas kernels  131 us (99%)
    pallas_call x1, Pallas kernels, local(): pl.pallas_call(main_kernel, out_shape=[jax.ShapeDtypeStruct((rows, points...  128 us
    pallas_call x1, Pallas kernels, local(): pl.pallas_call(finish_kernel, out_shape=[jax.ShapeDtypeStruct(dat.shape,...  3.02 us

profile of v6, /device:TPU:8, one launch (start us, length us, event | category | flops | bytes accessed | tf_op | source)
XLA Modules:
  0.0 131.3 jit_solution(11700905706555798224)
XLA Ops:
  0.6 127.6 %shard_map.179 = (bf16[64,5760]{1,0:T(8,128)(2,1)}, bf16[32,128,128]{2,1,0:T(8,128)(2,1)}, bf16[1536,128]{1,0:T(8,128)(2,1)}) custom-call(s32[1,45]{1,0:T(1,128)} %bitcast.15, f32[3,1,64]{2,1,0:T(1,128)} %bitcast.14, s32[45,128]{1,0:T(8,128)} %bitcast.13, bf16[64,5760]{1,0:T(8,128)(2,1)} %atmos_all.1, bf16[256,256]{1,0:T(8,128)(2,1)} %bitcast.11, ...), custom_call_target="tpu_custom_call" | custom-call | tf_op jit(solution)/shard_map/pallas_call | solution.py:692
  128.3 3.0 %shard_map.180 = (bf16[64,5760]{1,0:T(8,128)(2,1)}, f32[3,1,64]{2,1,0:T(1,128)}, f32[256,256]{1,0:T(8,128)}, f32[256,256]{1,0:T(8,128)}, f32[64,128]{1,0:T(8,128...) custom-call(bf16[64,5760]{1,0:T(8,128)(2,1)} %get-tuple-element.19.dat, ...), custom_call_target="tpu_custom_call" | custom-call | tf_op jit(solution)/shard_map/pallas_call | solution.py:767

commit v7 on v6

--- a/solution.py
+++ b/solution.py
@@ -109,7 +109,7 @@
     dat_all, dst, out,
     tabv, table, atmos, dat, al, cl, ext, zb, alm, tapt, tapr, tapf, w1, w2, wf, fx, fm, mk, mk4, hid, slope,
     ctv0, ctb, sp, rf, bk, rb, st, ctv, ds, wa, wb, perm, go1, go2,
-    dfp, dfb, gb, dext, dl, dq, dzacc, dubuf, gwf, gkp, gkr,
+    dfp, dfb, gb, dext, dl, dq, dubuf, gwf, gkp, gkr,
     gs, ra, hx, rw, gso, rao, hxo, rxo, own, owno, ownb, ownob, t, r1, fs, r2, fr, ag, tb,
     lsem, msem, hs, hr, ws, wr, ts, tr, as_, ar, fxs, fxr, cs, cr, ss, sr, rs, rr,
     os_, or_, dfs, dfr, h2s, h2r, gks, gkq, das, dar, s0, q0, s1, q1, s2, q2, s3, q3, s4, q4,
@@ -347,14 +347,11 @@
     for copy in fcopies:
         copy.wait()
 
-    def pack(s, _):
-        sp[s] = fm[table[0, s]]
-        return 0
-
-    lax.fori_loop(0, 2 * bands, pack, 0)
 
     def couple(n, ways):
         base = column(n, 1) * ZLEN
+        for i in range(span):
+            sp[2 * base + i] = fm[table[0, 2 * base + i]]
         for way in ways:
             to = base + way
             send(sp.at[pl.ds(2 * to, 2)], rf.at[pl.ds(2 * b, 2)], ss, sr.at[n], to, c)
@@ -472,34 +469,13 @@
     gwf[...] = nn(alm[...], dfb[...].reshape(share, PTS))
     wcopies = []
     halo = []
-    for turn, i in enumerate((mate, c, diag, across)):
-        for r in (0, 3, 1, 2):
+    for turn, i in enumerate((mate, diag, c, across)):
+        for r in range(lats):
             cols = slice(r * width, (r + 1) * width)
-            du = (nn(w2[i], gb[:, cols]) * slope[i, :, cols].astype(F32)).astype(BF16)
-            dubuf[:, cols] = du
-            piece = nn(w1[i], du)
-            if turn == 0:
-                dzacc[:, cols] = piece
-            elif turn < 3:
-                dzacc[:, cols] += piece
-            else:
-                at = (r + 1) * width
-                dext[:, at : at + width] = (dzacc[:, cols] + piece).astype(BF16)
-                if r == 0:
-                    halo.append(
-                        send(
-                            dext.at[:, at : at + width], dext.at[:, (lats + 1) * width :],
-                            h2s.at[1], h2r.at[1], up, c,
-                        )
-                    )
-                if r == 3:
-                    halo.append(
-                        send(
-                            dext.at[:, at : at + width], dext.at[:, :width],
-                            h2s.at[0], h2r.at[0], down, c,
-                        )
-                    )
-        g1 = nt(zb[...], dubuf[...])
+            dubuf[i, :, cols] = (
+                nn(w2[i], gb[:, cols]) * slope[i, :, cols].astype(F32)
+            ).astype(BF16)
+        g1 = nt(zb[...], dubuf[i])
         g2 = nt(hid[i], gb[...])
         for j in range(2):
             gs[i, j * 256 : j * 256 + 256] = g1[:, j * 128 : j * 128 + 128].astype(BF16)
@@ -508,17 +484,39 @@
         if turn == 0:
             mcopies = [send(gs.at[mate], ra.at[0], s0.at[0], q0.at[0], b, mate)]
         if turn == 1:
+            mcopies.append(send(gs.at[diag], ra.at[1], s0.at[1], q0.at[1], b, mate))
+        if turn == 2:
             mcopies[0].wait()
             own[...] = gs[c].astype(F32) + ra[0].astype(F32)
             ownb[...] = own[sent_big].astype(BF16)
             wcopies.append(send(ownb, rw.at[2], s0.at[4], q0.at[4], flip, c))
-        if turn == 2:
-            mcopies.append(send(gs.at[diag], ra.at[1], s0.at[1], q0.at[1], b, mate))
         if turn == 3:
             mcopies[1].wait()
             hx[...] = (gs[across].astype(F32) + ra[1].astype(F32)).astype(BF16)
             wcopies.append(send(hx.at[kept_big], rw.at[0], s0.at[2], q0.at[2], b, across))
             wcopies.append(send(hx.at[sent_big], rw.at[1], s0.at[3], q0.at[3], flip, across))
+    for r in (0, 3, 1, 2):
+        cols = slice(r * width, (r + 1) * width)
+        total = None
+        for i in range(4):
+            piece = nn(w1[i], dubuf[i, :, cols])
+            total = piece if total is None else total + piece
+        at = (r + 1) * width
+        dext[:, at : at + width] = total.astype(BF16)
+        if r == 0:
+            halo.append(
+                send(
+                    dext.at[:, at : at + width], dext.at[:, (lats + 1) * width :],
+                    h2s.at[1], h2r.at[1], up, c,
+                )
+            )
+        if r == 3:
+            halo.append(
+                send(
+                    dext.at[:, at : at + width], dext.at[:, :width],
+                    h2s.at[0], h2r.at[0], down, c,
+                )
+            )
     gkp[...] = jnp.zeros(gkp.shape, F32)
     for i in range(3):
         acc = jnp.zeros((full, 128), F32)
@@ -725,8 +723,7 @@
             VMEM((PTS, total), F32),
             VMEM((blocks, quarter, PTS), BF16),
             grouped, square, extended, square, split,
-            VMEM((full, share), F32),
-            VMEM((hid, share), BF16),
+            VMEM((chans, hid, share), BF16),
             VMEM((full, PTS), F32),
             VMEM((chans, 16, 128), F32),
             VMEM((chans, 16, 128), F32),

time: 132 us -> 133 us (level)
  no operation moved by 1% of the time
where the time goes in v7:
time: 133 us; the launch traced here: 132 us
  Pallas kernels  131 us (98%)
    pallas_call x1, Pallas kernels, local(): pl.pallas_call(main_kernel, out_shape=[jax.ShapeDtypeStruct((rows, points...  128 us
    pallas_call x1, Pallas kernels, local(): pl.pallas_call(finish_kernel, out_shape=[jax.ShapeDtypeStruct(dat.shape,...  3.02 us

profile of v7, /device:TPU:8, one launch (start us, length us, event | category | flops | bytes accessed | tf_op | source)
XLA Modules:
  0.0 131.5 jit_solution(18441839870234912966)
XLA Ops:
  0.6 127.8 %shard_map.179 = (bf16[64,5760]{1,0:T(8,128)(2,1)}, bf16[32,128,128]{2,1,0:T(8,128)(2,1)}, bf16[1536,128]{1,0:T(8,128)(2,1)}) custom-call(s32[1,45]{1,0:T(1,128)} %bitcast.15, f32[3,1,64]{2,1,0:T(1,128)} %bitcast.14, s32[45,128]{1,0:T(8,128)} %bitcast.13, bf16[64,5760]{1,0:T(8,128)(2,1)} %atmos_all.1, bf16[256,256]{1,0:T(8,128)(2,1)} %bitcast.11, ...), custom_call_target="tpu_custom_call" | custom-call | tf_op jit(solution)/shard_map/pallas_call | solution.py:690
  128.5 3.0 %shard_map.180 = (bf16[64,5760]{1,0:T(8,128)(2,1)}, f32[3,1,64]{2,1,0:T(1,128)}, f32[256,256]{1,0:T(8,128)}, f32[256,256]{1,0:T(8,128)}, f32[64,128]{1,0:T(8,128...) custom-call(bf16[64,5760]{1,0:T(8,128)(2,1)} %get-tuple-element.19.dat, ...), custom_call_target="tpu_custom_call" | custom-call | tf_op jit(solution)/shard_map/pallas_call | solution.py:764

commit v8 on v6

--- a/solution.py
+++ b/solution.py
@@ -347,14 +347,11 @@
     for copy in fcopies:
         copy.wait()
 
-    def pack(s, _):
-        sp[s] = fm[table[0, s]]
-        return 0
-
-    lax.fori_loop(0, 2 * bands, pack, 0)
 
     def couple(n, ways):
         base = column(n, 1) * ZLEN
+        for i in range(span):
+            sp[2 * base + i] = fm[table[0, 2 * base + i]]
         for way in ways:
             to = base + way
             send(sp.at[pl.ds(2 * to, 2)], rf.at[pl.ds(2 * b, 2)], ss, sr.at[n], to, c)
@@ -373,7 +370,16 @@
             ).astype(BF16)
     ctcopies = []
     for d, to in pairs:
-        ctcopies.append(send(cl.at[to], ctb.at[mine, :], cs.at[d], cr.at[d], b, to))
+        ctcopies.append(
+            pltpu.make_async_remote_copy(
+                src_ref=cl.at[to],
+                dst_ref=ctb.at[mine, :],
+                send_sem=cs.at[d],
+                recv_sem=cr.at[d],
+                device_id=(b, to),
+                device_id_type=MESH,
+            )
+        )
     ctb[mine, :] = cl[c]
 
     def step(n, _):
@@ -384,6 +390,11 @@
         @pl.when(n == groups - 1)
         def _():
             drain(rf.at[pl.ds(0, span - 2)], sr.at[n])
+
+        @pl.when(n == groups // 2)
+        def _():
+            for copy in ctcopies:
+                copy.start()
 
         src = column(n, -1)
         at = pl.ds(pl.multiple_of(src * span, span), span)

time: 132 us -> 134 us (1.015)
  no operation moved by 1% of the time
where the time goes in v8:
time: 134 us; the launch traced here: 133 us
  Pallas kernels  132 us (99%)
    pallas_call x1, Pallas kernels, local(): pl.pallas_call(main_kernel, out_shape=[jax.ShapeDtypeStruct((rows, points...  129 us
    pallas_call x1, Pallas kernels, local(): pl.pallas_call(finish_kernel, out_shape=[jax.ShapeDtypeStruct(dat.shape,...  3.02 us

profile of v8, /device:TPU:8, one launch (start us, length us, event | category | flops | bytes accessed | tf_op | source)
XLA Modules:
  0.0 132.6 jit_solution(6821882475206581420)
XLA Ops:
  0.6 128.9 %shard_map.179 = (bf16[64,5760]{1,0:T(8,128)(2,1)}, bf16[32,128,128]{2,1,0:T(8,128)(2,1)}, bf16[1536,128]{1,0:T(8,128)(2,1)}) custom-call(s32[1,45]{1,0:T(1,128)} %bitcast.15, f32[3,1,64]{2,1,0:T(1,128)} %bitcast.14, s32[45,128]{1,0:T(8,128)} %bitcast.13, bf16[64,5760]{1,0:T(8,128)(2,1)} %atmos_all.1, bf16[256,256]{1,0:T(8,128)(2,1)} %bitcast.11, ...), custom_call_target="tpu_custom_call" | custom-call | tf_op jit(solution)/shard_map/pallas_call | solution.py:703
  129.5 3.0 %shard_map.180 = (bf16[64,5760]{1,0:T(8,128)(2,1)}, f32[3,1,64]{2,1,0:T(1,128)}, f32[256,256]{1,0:T(8,128)}, f32[256,256]{1,0:T(8,128)}, f32[64,128]{1,0:T(8,128...) custom-call(bf16[64,5760]{1,0:T(8,128)(2,1)} %get-tuple-element.19.dat, ...), custom_call_target="tpu_custom_call" | custom-call | tf_op jit(solution)/shard_map/pallas_call | solution.py:778
